TPU v7x, 32 devices: a whole 2x2x4 slice. The times are simulated.
32 devices in a mesh: dp: 8 (over y, x, core), tensor: 4 (over z).
Axes of the slice: x: 2, y: 2, z: 4, core: 2. Of those that a mesh axis runs over, the one named last changes fastest.
Arguments:
- activations: bfloat16 [16384, 1536], P('dp'), may hold values from -6 to 6
- cotangent: bfloat16 [16384, 1536], P('dp'), may hold values from -11 to 11
- in_weight: float32 [1536, 2, 3072], P('dp', None, 'tensor'), may hold values from -0.15947199 to 0.15947199
- in_first: float32 [1536, 2, 3072], P('dp', None, 'tensor'), may hold values from -64 to 64
- in_second: float32 [1536, 2, 3072], P('dp', None, 'tensor'), may hold values from 491.52 to 1966.08
- step_weight: float32 [1536, 48], P('dp', 'tensor'), may hold values from -0.15625 to 0.15625
- step_first: float32 [1536, 48], P('dp', 'tensor'), may hold values from -64 to 64
- step_second: float32 [1536, 48], P('dp', 'tensor'), may hold values from 491.52 to 1966.08
- out_weight: float32 [3072, 1536], P('tensor', 'dp'), may hold values from -0.109375 to 0.109375
- out_first: float32 [3072, 1536], P('tensor', 'dp'), may hold values from -64 to 64
- out_second: float32 [3072, 1536], P('tensor', 'dp'), may hold values from 491.52 to 1966.08
- state_weight: float32 [1536, 256], P(('dp', 'tensor')), may hold values from -0.15625 to 0.15625
- state_first: float32 [1536, 256], P(('dp', 'tensor')), may hold values from -64 to 64
- state_second: float32 [1536, 256], P(('dp', 'tensor')), may hold values from 491.52 to 1966.08
- conv_weight: float32 [4, 3328], P(None, ('dp', 'tensor')), may hold values from -3 to 3
- conv_first: float32 [4, 3328], P(None, ('dp', 'tensor')), may hold values from -80 to 80
- conv_second: float32 [4, 3328], P(None, ('dp', 'tensor')), may hold values from 819.2 to 3276.8
- conv_bias: float32 [3328], P(('dp', 'tensor')), may hold values from -3 to 3
- bias_first: float32 [3328], P(('dp', 'tensor')), may hold values from -80 to 80
- bias_second: float32 [3328], P(('dp', 'tensor')), may hold values from 819.2 to 3276.8
- gain_vector: float32 [4608], P(('dp', 'tensor')), may hold values from 0.5 to 1.5
- gains_first: float32 [4608], P(('dp', 'tensor')), may hold values from -80 to 80
- gains_second: float32 [4608], P(('dp', 'tensor')), may hold values from 819.2 to 3276.8
- head_params: float32 [3, 48], replicated, may hold values from -6 to 1.5, as said below
- head_first: float32 [3, 48], replicated, may hold values from -80 to 80
- head_second: float32 [3, 48], replicated, may hold values from 819.2 to 3276.8
Outputs:
- block_output: bfloat16 [16384, 1536], P('dp')
- input_grad: float32 [16384, 1536], P('dp')
- in_updated: float32 [1536, 2, 3072], P('dp', None, 'tensor')
- in_moment: float32 [1536, 2, 3072], P('dp', None, 'tensor')
- in_square: float32 [1536, 2, 3072], P('dp', None, 'tensor')
- step_updated: float32 [1536, 48], P('dp', 'tensor')
- step_moment: float32 [1536, 48], P('dp', 'tensor')
- step_square: float32 [1536, 48], P('dp', 'tensor')
- out_updated: float32 [3072, 1536], P('tensor', 'dp')
- out_moment: float32 [3072, 1536], P('tensor', 'dp')
- out_square: float32 [3072, 1536], P('tensor', 'dp')
- state_updated: float32 [1536, 256], P(('dp', 'tensor'))
- state_moment: float32 [1536, 256], P(('dp', 'tensor'))
- state_square: float32 [1536, 256], P(('dp', 'tensor'))
- conv_updated: float32 [4, 3328], P(None, ('dp', 'tensor'))
- conv_moment: float32 [4, 3328], P(None, ('dp', 'tensor'))
- conv_square: float32 [4, 3328], P(None, ('dp', 'tensor'))
- bias_updated: float32 [3328], P(('dp', 'tensor'))
- bias_moment: float32 [3328], P(('dp', 'tensor'))
- bias_square: float32 [3328], P(('dp', 'tensor'))
- gains_updated: float32 [4608], P(('dp', 'tensor'))
- gains_moment: float32 [4608], P(('dp', 'tensor'))
- gains_square: float32 [4608], P(('dp', 'tensor'))
- head_updated: float32 [3, 48], replicated
- head_moment: float32 [3, 48], replicated
- head_square: float32 [3, 48], replicated
Inputs may be any that keep to these rules, and one draw needn't show every extreme that they name: `head_params`: row 0 the logarithms of the decay rates, row 1 the biases of the step sizes, row 2 the skip factors.
All inputs are finite; a program needn't handle non-finite values.
Results may differ from a plain program's by a relative error of at most 0.03.
Values may be sent and summed in bfloat16 or wider, within the bound.
A program may use at most 256 MiB of HBM per device.

v0:
```python
import jax
import jax.numpy as jnp
from jax import lax
from jax.sharding import PartitionSpec as P

D = 1536
SPAN = 256
LENGTH = 1024
STEP = 5
INNER = 3072


HIGHEST = lax.Precision.HIGHEST
NORM_EPSILON = 1e-05
FIRST_DECAY = 0.9
SECOND_DECAY = 0.95
ADAM_EPSILON = 1e-08
WEIGHT_DECAY = 0.1
RATE_MATRIX = 0.05
RATE_OUTPUT = 0.04
RATE_CONV = 1.0
RATE_VECTOR = 0.5
RATE_HEADS = 2.0


def causal_conv(values, kernel, offsets):
    length = values.shape[0]
    tap_count = kernel.shape[0]
    padded = jnp.pad(values, ((tap_count - 1, 0), (0, 0)))
    result = offsets[None, :] + kernel[0][None, :] * padded[0:length]
    for shift_tap in range(1, tap_count):
        result = result + kernel[shift_tap][None, :] * padded[shift_tap : shift_tap + length]
    return result


def state_space(values, step_sizes, decay_rates, inputs_b, inputs_c):
    length, head_count, head_width = values.shape
    block_count = length // SPAN
    causal_mask = lax.broadcasted_iota(jnp.int32, (SPAN, SPAN), 0) >= lax.broadcasted_iota(
        jnp.int32, (SPAN, SPAN), 1
    )

    def one_block(carry_state, block_piece):
        block_values, block_steps, block_b, block_c = block_piece
        decays = (block_steps * decay_rates[None, :]).T
        totals = jnp.cumsum(decays, axis=1)
        decay_gaps = jnp.where(
            causal_mask[None, :, :], totals[:, :, None] - totals[:, None, :], -10000.0
        )
        intersection = jnp.dot(block_c, block_b.T, precision=HIGHEST)
        mixing = jnp.exp(decay_gaps) * intersection[None, :, :] * block_steps.T[:, None, :]
        within = jnp.einsum("hts,shp->thp", mixing, block_values, precision=HIGHEST)
        carried = jnp.exp(totals).T[:, :, None] * jnp.einsum(
            "tn,hpn->thp", block_c, carry_state, precision=HIGHEST
        )
        block_ends = totals[:, -1]
        weights = (jnp.exp(block_ends[:, None] - totals) * block_steps.T).T
        fresh_state = jnp.einsum(
            "shp,sn->hpn", weights[:, :, None] * block_values, block_b, precision=HIGHEST
        )
        return (jnp.exp(block_ends)[:, None, None] * carry_state + fresh_state, within + carried)

    pieces = (
        values.reshape(block_count, SPAN, head_count, head_width),
        step_sizes.reshape(block_count, SPAN, head_count),
        inputs_b.reshape(block_count, SPAN, inputs_b.shape[1]),
        inputs_c.reshape(block_count, SPAN, inputs_c.shape[1]),
    )
    initial = jnp.zeros((head_count, head_width, inputs_b.shape[1]), jnp.float32)
    _, outputs = lax.scan(jax.checkpoint(one_block), initial, pieces)
    return outputs.reshape(length, head_count, head_width)


def mix_sequence(gate_in, value_in, state_in, step_in, kernel, offsets, head_table, gain_row):
    length = gate_in.shape[0]
    inner_width = value_in.shape[1]
    head_count = head_table.shape[1]
    states = state_in.shape[1] // 2
    active = jax.nn.silu(causal_conv(jnp.concatenate([value_in, state_in], 1), kernel, offsets))
    channels = active[:, :inner_width].reshape(length, head_count, inner_width // head_count)
    step_sizes = jax.nn.softplus(step_in + head_table[1][None, :])
    decay_rates = -jnp.exp(head_table[0])
    output = state_space(
        channels,
        step_sizes,
        decay_rates,
        active[:, inner_width : inner_width + states],
        active[:, inner_width + states :],
    )
    output = output + head_table[2][None, :, None] * channels
    gated_out = output.reshape(length, inner_width) * jax.nn.silu(gate_in)
    return (gated_out * gain_row[None, :], jnp.sum(gated_out * gated_out, axis=1, keepdims=True))


def mixer_local(gate_in, value_in, state_in, step_in, kernel, offsets, head_table, gain_row):
    sequences = gate_in.shape[0] // LENGTH

    def per_sequence(gate_seq, value_seq, state_seq, step_seq):
        return mix_sequence(
            gate_seq, value_seq, state_seq, step_seq, kernel, offsets, head_table, gain_row
        )

    gated_out, squares = jax.vmap(per_sequence)(
        gate_in.reshape(sequences, LENGTH, gate_in.shape[1]),
        value_in.reshape(sequences, LENGTH, value_in.shape[1]),
        state_in.reshape(sequences, LENGTH, state_in.shape[1]),
        step_in.reshape(sequences, LENGTH, step_in.shape[1]),
    )
    return (gated_out.reshape(-1, gated_out.shape[2]), squares.reshape(-1, 1))


def prenorm(values, gain_row):
    return (
        values
        * lax.rsqrt(jnp.mean(values * values, axis=1, keepdims=True) + NORM_EPSILON)
        * gain_row[None, :]
    )


def product(operand, factor):
    return jnp.dot(operand, factor, preferred_element_type=jnp.float32)


def product_left(operand, factor):
    return lax.dot_general(
        operand, factor, (((0,), (0,)), ((), ())), preferred_element_type=jnp.float32
    )


def product_right(operand, factor):
    return lax.dot_general(
        operand, factor, (((1,), (1,)), ((), ())), preferred_element_type=jnp.float32
    )


def norm_rows(values, back_grad, branch, squares_total):
    norm_scale = lax.rsqrt(squares_total / INNER + NORM_EPSILON)
    block_values = values + norm_scale * branch
    branch_grad = (norm_scale * back_grad).astype(jnp.bfloat16)
    scale_grad = jnp.sum(back_grad * branch, axis=1, keepdims=True)
    squares_grad = -0.5 * scale_grad * norm_scale * norm_scale * norm_scale / INNER
    return (block_values.astype(jnp.bfloat16), branch_grad, squares_grad)


def adamw_update(weight, gradient, moment, square, step_rate, decay_rate):
    moment = FIRST_DECAY * moment + (1.0 - FIRST_DECAY) * gradient
    square = SECOND_DECAY * square + (1.0 - SECOND_DECAY) * gradient * gradient
    first_fix = 1.0 - FIRST_DECAY**STEP
    second_fix = 1.0 - SECOND_DECAY**STEP
    update = moment / first_fix / (jnp.sqrt(square / second_fix) + ADAM_EPSILON)
    return (weight - step_rate * (update + decay_rate * weight), moment, square)


def shards(
    activations,
    cotangent,
    in_weight,
    in_first,
    in_second,
    step_weight,
    step_first,
    step_second,
    out_weight,
    out_first,
    out_second,
    state_weight,
    state_first,
    state_second,
    conv_weight,
    conv_first,
    conv_second,
    conv_bias,
    bias_first,
    bias_second,
    gain_vector,
    gains_first,
    gains_second,
    head_params,
    head_first,
    head_second,
):
    tensor_rank = lax.axis_index("tensor")
    in_rows, step_rows, out_rows = (
        lax.all_gather(in_weight.astype(jnp.bfloat16), "dp", axis=0, tiled=True),
        lax.all_gather(step_weight.astype(jnp.bfloat16), "dp", axis=0, tiled=True),
        lax.all_gather(out_weight.astype(jnp.bfloat16), "dp", axis=1, tiled=True),
    )
    state_full, kernel_full, offsets_full, gains_full = (
        lax.all_gather(state_weight, ("dp", "tensor"), axis=0, tiled=True),
        lax.all_gather(conv_weight, ("dp", "tensor"), axis=1, tiled=True),
        lax.all_gather(conv_bias, ("dp", "tensor"), axis=0, tiled=True),
        lax.all_gather(gain_vector, ("dp", "tensor"), axis=0, tiled=True),
    )
    inner_local = in_rows.shape[2]
    heads_local = step_rows.shape[1]
    inner_start = tensor_rank * inner_local
    kernel_local = jnp.concatenate(
        [
            lax.dynamic_slice_in_dim(kernel_full, inner_start, inner_local, 1),
            kernel_full[:, INNER:],
        ],
        1,
    )
    offsets_local = jnp.concatenate(
        [lax.dynamic_slice_in_dim(offsets_full, inner_start, inner_local, 0), offsets_full[INNER:]],
        0,
    )
    gain_local = lax.dynamic_slice_in_dim(gains_full, D + inner_start, inner_local, 0)
    head_local = lax.dynamic_slice_in_dim(head_params, tensor_rank * heads_local, heads_local, 1)
    state_low = state_full.astype(jnp.bfloat16)
    in_matrix = in_rows.reshape(D, 2 * inner_local)
    values = activations.astype(jnp.float32)
    normed, norm_pull = jax.vjp(prenorm, values, gains_full[:D])
    normed_low = normed.astype(jnp.bfloat16)
    gate_value = product(normed_low, in_matrix)
    state_in = product(normed_low, state_low)
    step_in = product(normed_low, step_rows)
    (gated_out, squares), mixer_pull = jax.vjp(
        mixer_local,
        gate_value[:, :inner_local],
        gate_value[:, inner_local:],
        state_in,
        step_in,
        kernel_local,
        offsets_local,
        head_local,
        gain_local,
    )
    gated_low = gated_out.astype(jnp.bfloat16)
    back_grad = cotangent.astype(jnp.float32)
    head_terms = product(gated_low, out_rows)
    branch, squares_total = (
        lax.psum(head_terms.astype(jnp.bfloat16), "tensor").astype(jnp.float32),
        lax.psum(squares.astype(jnp.bfloat16), "tensor").astype(jnp.float32),
    )
    output_low, branch_grad, squares_grad = norm_rows(values, back_grad, branch, squares_total)
    out_grad = product_left(gated_low, branch_grad)
    gated_grad = product_right(branch_grad, out_rows)
    (
        gate_grad,
        value_grad,
        state_grad,
        step_grad,
        kernel_grad,
        offsets_grad,
        head_grad,
        gain_grad,
    ) = mixer_pull((gated_grad, squares_grad))
    in_grad_low = jnp.concatenate([gate_grad, value_grad], 1).astype(jnp.bfloat16)
    state_grad_low = state_grad.astype(jnp.bfloat16)
    step_grad_low = step_grad.astype(jnp.bfloat16)
    in_wgrad = product_left(normed_low, in_grad_low).reshape(D, 2, inner_local)
    state_wgrad = product_left(normed_low, state_grad_low)
    step_wgrad = product_left(normed_low, step_grad_low)
    normed_grad = (
        product_right(in_grad_low, in_matrix)
        + product_right(state_grad_low, state_low)
        + product_right(step_grad_low, step_rows)
    )
    input_part, pre_gain_grad = norm_pull(normed_grad)
    input_grad = lax.psum(input_part.astype(jnp.bfloat16), "tensor").astype(jnp.float32) + back_grad
    in_owned, step_owned, out_owned = (
        lax.psum_scatter(
            in_wgrad.astype(jnp.bfloat16), "dp", scatter_dimension=0, tiled=True
        ).astype(jnp.float32),
        lax.psum_scatter(
            step_wgrad.astype(jnp.bfloat16), "dp", scatter_dimension=0, tiled=True
        ).astype(jnp.float32),
        lax.psum_scatter(
            out_grad.astype(jnp.bfloat16), "dp", scatter_dimension=1, tiled=True
        ).astype(jnp.float32),
    )
    kernel_grad_full = jnp.zeros(kernel_full.shape, jnp.float32)
    kernel_grad_full = lax.dynamic_update_slice_in_dim(
        kernel_grad_full, kernel_grad[:, :inner_local], inner_start, 1
    )
    kernel_grad_full = lax.dynamic_update_slice_in_dim(
        kernel_grad_full, kernel_grad[:, inner_local:], INNER, 1
    )
    offsets_grad_full = jnp.zeros(offsets_full.shape, jnp.float32)
    offsets_grad_full = lax.dynamic_update_slice_in_dim(
        offsets_grad_full, offsets_grad[:inner_local], inner_start, 0
    )
    offsets_grad_full = lax.dynamic_update_slice_in_dim(
        offsets_grad_full, offsets_grad[inner_local:], INNER, 0
    )
    gains_grad_full = jnp.concatenate([pre_gain_grad, jnp.zeros((INNER,), jnp.float32)], 0)
    gains_grad_full = lax.dynamic_update_slice_in_dim(
        gains_grad_full, gain_grad, D + inner_start, 0
    )
    head_grad_full = jnp.zeros(head_params.shape, jnp.float32)
    head_grad_full = lax.dynamic_update_slice_in_dim(
        head_grad_full, head_grad, tensor_rank * heads_local, 1
    )
    state_owned, kernel_owned, offsets_owned, gains_owned = (
        lax.psum_scatter(state_wgrad, ("dp", "tensor"), scatter_dimension=0, tiled=True),
        lax.psum_scatter(kernel_grad_full, ("dp", "tensor"), scatter_dimension=1, tiled=True),
        lax.psum_scatter(offsets_grad_full, ("dp", "tensor"), scatter_dimension=0, tiled=True),
        lax.psum_scatter(gains_grad_full, ("dp", "tensor"), scatter_dimension=0, tiled=True),
    )
    head_total = lax.psum(head_grad_full, ("dp", "tensor"))
    in_new = adamw_update(in_weight, in_owned, in_first, in_second, RATE_MATRIX, WEIGHT_DECAY)
    step_new = adamw_update(
        step_weight, step_owned, step_first, step_second, RATE_MATRIX, WEIGHT_DECAY
    )
    out_new = adamw_update(out_weight, out_owned, out_first, out_second, RATE_OUTPUT, WEIGHT_DECAY)
    state_new = adamw_update(
        state_weight, state_owned, state_first, state_second, RATE_MATRIX, WEIGHT_DECAY
    )
    conv_new = adamw_update(conv_weight, kernel_owned, conv_first, conv_second, RATE_CONV, 0.0)
    bias_new = adamw_update(conv_bias, offsets_owned, bias_first, bias_second, RATE_VECTOR, 0.0)
    gains_new = adamw_update(gain_vector, gains_owned, gains_first, gains_second, RATE_VECTOR, 0.0)
    head_new = adamw_update(head_params, head_total, head_first, head_second, RATE_HEADS, 0.0)
    return (
        output_low,
        input_grad,
        in_new[0],
        in_new[1],
        in_new[2],
        step_new[0],
        step_new[1],
        step_new[2],
        out_new[0],
        out_new[1],
        out_new[2],
        state_new[0],
        state_new[1],
        state_new[2],
        conv_new[0],
        conv_new[1],
        conv_new[2],
        bias_new[0],
        bias_new[1],
        bias_new[2],
        gains_new[0],
        gains_new[1],
        gains_new[2],
        head_new[0],
        head_new[1],
        head_new[2],
    )


def solution(mesh):
    return jax.shard_map(
        shards,
        mesh=mesh,
        in_specs=(
            P("dp", None),
            P("dp", None),
            P("dp", None, "tensor"),
            P("dp", None, "tensor"),
            P("dp", None, "tensor"),
            P("dp", "tensor"),
            P("dp", "tensor"),
            P("dp", "tensor"),
            P("tensor", "dp"),
            P("tensor", "dp"),
            P("tensor", "dp"),
            P(("dp", "tensor"), None),
            P(("dp", "tensor"), None),
            P(("dp", "tensor"), None),
            P(None, ("dp", "tensor")),
            P(None, ("dp", "tensor")),
            P(None, ("dp", "tensor")),
            P(("dp", "tensor")),
            P(("dp", "tensor")),
            P(("dp", "tensor")),
            P(("dp", "tensor")),
            P(("dp", "tensor")),
            P(("dp", "tensor")),
            P(),
            P(),
            P(),
        ),
        out_specs=(
            P("dp", None),
            P("dp", None),
            P("dp", None, "tensor"),
            P("dp", None, "tensor"),
            P("dp", None, "tensor"),
            P("dp", "tensor"),
            P("dp", "tensor"),
            P("dp", "tensor"),
            P("tensor", "dp"),
            P("tensor", "dp"),
            P("tensor", "dp"),
            P(("dp", "tensor"), None),
            P(("dp", "tensor"), None),
            P(("dp", "tensor"), None),
            P(None, ("dp", "tensor")),
            P(None, ("dp", "tensor")),
            P(None, ("dp", "tensor")),
            P(("dp", "tensor")),
            P(("dp", "tensor")),
            P(("dp", "tensor")),
            P(("dp", "tensor")),
            P(("dp", "tensor")),
            P(("dp", "tensor")),
            P(),
            P(),
            P(),
        ),
        check_vma=False,
    )
```

profile of v0, /device:TPU:0, one launch (start us, length us, event | category | flops | bytes accessed | tf_op | source)
XLA Modules:
  0.0 1871.5 jit_solution(18105247608557594733)
XLA Ops:
  11.6 42.7 %all-reduce.24 = (f32[4608]{0:T(1024)S(1)}, f32[3328]{0:T(1024)S(1)}) all-reduce(f32[4608]{0:T(1024)S(1)} %dynamic-update-slice, f32[3328]{0:T(1024)S(1)} %dynamic-update-slice.1), channel_id=1, replica_groups=mesh['dp'=8,'tensor'=4] {'dp','tensor'}, use_global_device_ids=true, to_apply=%add.17 | all-reduce | flops 7936 | bytes 63488
  55.2 66.6 %all-gather.1 = f32[32,104,4]{1,2,0:T(4,128)S(1)} all-gather(f32[1,104,4]{1,2,0:T(4,128)} %bitcast.464), channel_id=1, replica_groups=mesh['dp'=8,'tensor'=4] {'dp','tensor'}, dimensions={0}, use_global_device_ids=true | all-gather | bytes 54912 | tf_op jit(solution)/shard_map/all_gather | solution.py:190
  147.1 72.1 %all_gather.26 = bf16[1536,256]{1,0:T(8,128)(2,1)S(1)} all-gather(bf16[48,256]{1,0:T(8,128)(2,1)S(1)} %convert.37), channel_id=1, replica_groups=mesh['dp'=8,'tensor'=4] {'dp','tensor'}, dimensions={0}, use_global_device_ids=true | all-gather | bytes 811008 | tf_op jit(solution)/shard_map/all_gather | solution.py:189
  231.5 14.7 fusion.168
  263.7 19.1 %fusion.108 = (f32[2,1024,1024]{2,1,0:T(8,128)}, f32[2,1024,1024]{2,1,0:T(8,128)}) fusion(f32[2,1024,1024]{2,1,0:T(8,128)} %pad_maximum_fusion, f32[1024]{0:T(1024)S(1)} %bitcast.444, f32[1024]{0:T(1024)S(1)} %bitcast.446, f32[1024]{0:T(1024)S(1)} %bitcast.442, f32[1024]{0:T(1024)S(1)} %bitcast.440, f32[1024]{0:T(1024)S(1)} %pad_maximum_fusion.5), kind=kLoop, calls=%fused_computation.164 | loop fusion | flops 25165824 | bytes 25186304 | tf_op jit(solution)/shard_map/jvp(vmap(jit(silu)))/mul | solution.py:79
  317.4 79.7 %while.41 = (s32[]{:T(128)}, f32[2,12,64,128]{3,2,1,0:T(8,128)S(1)}, f32[4,2,256,12,64]{2,4,3,1,0:T(8,128)}, f32[4,2,12,64,128]{4,3,2,1,0:T(8,128)}, f32[4,2,256...) while((s32[]{:T(128)}, ...), condition=%wide.region_4.5_spmd.clone, body=%wide.region_1.4_spmd.clone.sunk | while | flops 2626504704 | bytes 14776873 | solution.py:70
  445.2 12.7 convolution_convert_fusion.2
  458.0 39.7 %reduce-scatter.7.cloned.1.call-done = bf16[768,192]{0,1:T(8,128)(2,1)} async-done(((bf16[768,1536]{0,1:T(8,128)(2,1)}), bf16[768,192]{0,1:T(8,128)(2,1)}) %reduce-scatter.7.cloned.1.call-update) | async-done | bytes 294928 | tf_op jit(solution)/shard_map/reduce_scatter | solution.py:269
  501.1 29.1 %all-gather.7.cloned.1.call-done = bf16[768,1536]{0,1:T(8,128)(2,1)} async-done(((bf16[768,192]{0,1:T(8,128)(2,1)}), bf16[768,1536]{0,1:T(8,128)(2,1)}) %all-gather.7.cloned.1.call-update) | async-done | bytes 2359312 | tf_op jit(solution)/shard_map/all_gather | solution.py:186
  550.8 211.5 %all-reduce.30.cloned.1.call-done = bf16[2048,1536]{1,0:T(8,128)(2,1)} async-done(((bf16[2048,1536]{1,0:T(8,128)(2,1)}), bf16[2048,1536]{1,0:T(8,128)(2,1)}) %all-reduce.30.cloned.1.call-update) | async-done | bytes 6291472 | tf_op jit(solution)/shard_map/psum | solution.py:233
  768.6 16.5 multiply_reduce_fusion.9
  806.6 344.2 %while.42 = (s32[]{:T(128)}, f32[12]{0:T(128)}, f32[2,12,64,128]{3,2,1,0:T(8,128)}, f32[4,2,256,12,64]{2,4,3,1,0:T(8,128)}, f32[4,2,256,12]{3,1,2,0:T(2,128)}, /...) while((s32[]{:T(128)}, f32[12]{0:T(128)}, ...), condition=%wide.region_23.24_spmd.clone, body=%wide.region_9.0_spmd.clone.sunk | while | flops 6072801280 | bytes 50500788 | solution.py:70
  1183.4 17.1 multiply_reduce_fusion.7
  1215.8 13.1 add_convert_fusion
  1244.1 16.3 fusion.113
  1260.4 14.5 fusion.99
  1286.6 15.5 convolution_convert_fusion.1
  1302.1 12.6 copy.304
  1314.8 15.3 fusion.102
  1332.2 64.6 %all-reduce.36.cloned.1.call-done = (f32[4,3328]{1,0:T(4,128)}, f32[3328]{0:T(1024)}, f32[4608]{0:T(1024)}, f32[3,48]{1,0:T(4,128)}) async-done(((f32[4,3328]{1,0:T(4,128)}, f32[3328]{0:T(1024)}, f32[4608]{0:T(1024)}, f32[3,48]{1,0:T(4,128)}), (f32[4,3328]{1,0:T(4,128)}, f32[3328]{0:T(1024)}, f32[4608]{0:T(1024)}, f32[3,48]{1,0:T(4,128)})) %all-reduce.36.cloned.1.call-update) | async-done | bytes 85584
  1402.2 33.3 %reduce-scatter.11.cloned.1.call-done = bf16[192,12]{1,0:T(8,128)(2,1)} async-done(((bf16[1536,12]{1,0:T(8,128)(2,1)}), bf16[192,12]{1,0:T(8,128)(2,1)}) %reduce-scatter.11.cloned.1.call-update) | async-done | bytes 4624
  1438.4 100.3 %reduce-scatter.9.cloned.1.call-done = f32[48,256]{1,0:T(8,128)} async-done(((f32[1536,256]{1,0:T(8,128)}), f32[48,256]{1,0:T(8,128)}) %reduce-scatter.9.cloned.1.call-update) | async-done | bytes 49168 | tf_op jit(solution)/shard_map/reduce_scatter | solution.py:296
  1540.2 88.0 %all-reduce.34.cloned.1.call-done = bf16[1536,2,768]{2,1,0:T(2,128)(2,1)} async-done(((bf16[1536,2,768]{2,1,0:T(2,128)(2,1)}), bf16[1536,2,768]{2,1,0:T(2,128)(2,1)}) %all-reduce.34.cloned.1.call-update) | async-done | bytes 4718608
  1634.6 219.0 %all-reduce.32.cloned.1.call-done = bf16[2048,1536]{1,0:T(8,128)(2,1)} async-done(((bf16[2048,1536]{1,0:T(8,128)(2,1)}), bf16[2048,1536]{1,0:T(8,128)(2,1)}) %all-reduce.32.cloned.1.call-update) | async-done | bytes 6291472 | tf_op jit(solution)/shard_map/psum | solution.py:261
  (606 shorter events, 711.7 us)
Async XLA Ops:
  7.2 218.8 %all-gather.5.cloned.1.call-start = ((), (), s32[]{:S(2)}) async-start(), calls=%async_computation.3 | async-start | bytes 5308416 | tf_op jit(solution)/shard_map/all_gather | solution.py:184
  9.8 488.0 %reduce-scatter.7.cloned.1.call-start = ((), (), s32[]{:S(2)}) async-start(), calls=%async_computation.7 | async-start | bytes 2654208 | tf_op jit(solution)/shard_map/reduce_scatter | solution.py:269
  54.3 81.7 %copy-start.28 = (f32[1536]{0:T(1024)}, f32[1536]{0:T(1024)S(1)}, u32[]{:S(2)}) copy-start(f32[1536]{0:T(1024)S(1)} %slice.173) | copy-start | bytes 18436
  143.8 82.1 %copy-start.7 = (f32[2,4,256,12]{3,0,2,1:T(2,128)}, f32[2,4,256,12]{3,0,2,1:T(2,128)S(1)}, u32[]{:S(2)}) copy-start(f32[2,4,256,12]{3,0,2,1:T(2,128)S(1)} %copy.285) | copy-start | bytes 294916
  143.9 395.4 %copy-start.56 = (f32[3,12]{1,0:T(4,128)}, f32[3,12]{1,0:T(4,128)S(1)}, u32[]{:S(2)}) copy-start(f32[3,12]{1,0:T(4,128)S(1)} %constant_dynamic-slice_fusion.1) | copy-start | bytes 436
  146.3 79.7 %copy-start.6 = (f32[4,2,256,12]{3,1,2,0:T(2,128)}, f32[4,2,256,12]{3,1,2,0:T(2,128)S(1)}, u32[]{:S(2)}) copy-start(f32[4,2,256,12]{3,1,2,0:T(2,128)S(1)} %fusion.149) | copy-start | bytes 294916
  147.0 116.6 %copy-start.37 = (f32[1,1024]{1,0:T(1,128)}, f32[1,1024]{1,0:T(1,128)S(1)}, u32[]{:S(2)}) copy-start(f32[1,1024]{1,0:T(1,128)S(1)} %get-tuple-element.763) | copy-start | bytes 12292
  147.0 116.6 %copy-start.39 = (f32[1,1024]{1,0:T(1,128)}, f32[1,1024]{1,0:T(1,128)S(1)}, u32[]{:S(2)}) copy-start(f32[1,1024]{1,0:T(1,128)S(1)} %get-tuple-element.764) | copy-start | bytes 12292
  147.1 116.6 %copy-start.41 = (f32[1,1024]{1,0:T(1,128)}, f32[1,1024]{1,0:T(1,128)S(1)}, u32[]{:S(2)}) copy-start(f32[1,1024]{1,0:T(1,128)S(1)} %get-tuple-element.765) | copy-start | bytes 12292
  147.1 116.6 %copy-start.43 = (f32[1,1024]{1,0:T(1,128)}, f32[1,1024]{1,0:T(1,128)S(1)}, u32[]{:S(2)}) copy-start(f32[1,1024]{1,0:T(1,128)S(1)} %get-tuple-element.766) | copy-start | bytes 12292
  441.9 97.4 %copy-start.45 = (f32[2048,1]{0,1:T(1,128)}, f32[2048,1]{0,1:T(1,128)S(1)}, u32[]{:S(2)}) copy-start(f32[2048,1]{0,1:T(1,128)S(1)} %add_rsqrt_fusion) | copy-start | bytes 24580
  458.0 72.3 %all-gather.7.cloned.1.call-start = ((), (), s32[]{:S(2)}) async-start(), calls=%async_computation.4 | async-start | bytes 2654208 | tf_op jit(solution)/shard_map/all_gather | solution.py:186
  501.1 261.2 %all-reduce.30.cloned.1.call-start = ((), (), s32[]{:S(2)}) async-start(), calls=%async_computation.5 | async-start | bytes 12582912 | tf_op jit(solution)/shard_map/psum | solution.py:233
  539.3 857.5 %all-reduce.36.cloned.1.call-start = ((), (), s32[]{:S(2)}) async-start(), calls=%async_computation.11 | async-start | bytes 184320
  869.5 20.0 %copy-start.49 = (f32[12]{0:T(128)S(1)}, f32[12]{0:T(128)}, u32[]{:S(2)}) copy-start(f32[12]{0:T(128)} %get-tuple-element.1031) | copy-start | bytes 148 | tf_op jit(solution)/shard_map/transpose(jvp(vmap()))/while
  1240.0 20.4 %slice-start = ((s8[6291456]{0:T(1024)(128)(4,1)}), s8[2097152]{0:T(1024)(128)(4,1)S(1)}, s32[]{:S(2)}) async-start(s8[6291456]{0:T(1024)(128)(4,1)} %bitcast.406), calls=%async_computation.12 | async-start | bytes 4194304
  1275.9 159.6 %reduce-scatter.11.cloned.1.call-start = ((), (), s32[]{:S(2)}) async-start(), calls=%async_computation.9 | async-start | bytes 442368
  1280.7 258.0 %reduce-scatter.9.cloned.1.call-start = ((), (), s32[]{:S(2)}) async-start(), calls=%async_computation.8 | async-start | bytes 1622016 | tf_op jit(solution)/shard_map/reduce_scatter | solution.py:296
  1286.6 341.7 %all-reduce.34.cloned.1.call-start = ((), (), s32[]{:S(2)}) async-start(), calls=%async_computation.10 | async-start | bytes 9437184
  1314.7 538.9 %all-reduce.32.cloned.1.call-start = ((), (), s32[]{:S(2)}) async-start(), calls=%async_computation.6 | async-start | bytes 12582912 | tf_op jit(solution)/shard_map/psum | solution.py:261
  1330.1 106.9 %copy-start.35 = (f32[192,12]{0,1:T(8,128)S(1)}, f32[192,12]{0,1:T(8,128)}, u32[]{:S(2)}) copy-start(f32[192,12]{0,1:T(8,128)} %param.35) | copy-start | bytes 27652
  1330.1 298.1 %copy-start.15 = (f32[192,2,768]{2,1,0:T(2,128)S(1)}, f32[192,2,768]{2,1,0:T(2,128)}, u32[]{:S(2)}) copy-start(f32[192,2,768]{2,1,0:T(2,128)} %param.32) | copy-start | bytes 3538948
  1330.1 298.1 %copy-start.22 = (f32[192,2,768]{2,1,0:T(2,128)S(1)}, f32[192,2,768]{2,1,0:T(2,128)}, u32[]{:S(2)}) copy-start(f32[192,2,768]{2,1,0:T(2,128)} %param.33) | copy-start | bytes 3538948
  1330.1 298.1 %copy-start.23 = (f32[192,2,768]{2,1,0:T(2,128)S(1)}, f32[192,2,768]{2,1,0:T(2,128)}, u32[]{:S(2)}) copy-start(f32[192,2,768]{2,1,0:T(2,128)} %param.34) | copy-start | bytes 3538948
  (65 other events, 631.3 us)
Sparse Core Ops, SparseCore 0:
  10.5 41.9 all-gather.4
  458.1 39.6 reduce-scatter.6
  501.2 29.0 all-gather.6
  539.4 222.8 all-reduce.29
  1276.0 120.7 all-reduce.35
  1400.6 34.8 reduce-scatter.10
  1441.6 97.0 reduce-scatter.8
  1542.4 85.8 all-reduce.33
  1630.6 222.9 all-reduce.31
where the time goes:
time: 1880 us; the launch traced here: 1870 us
  waiting for transfers between devices  786 us (42%)
  matrix products  356 us (19%)
  local copies, waits for them, and re-layouts  257 us (14%)
  other arithmetic  248 us (13%)
  blocking collectives  199 us (11%)
    psum x1, waiting for transfers between devices, shards(): lax.psum(input_part.astype(jnp.bfloat16), 'tensor').astype(jnp.float32)  219 us
    psum x1, waiting for transfers between devices, shards(): lax.psum(head_terms.astype(jnp.bfloat16), 'tensor').astype(jnp.float32)  211 us
    unnamed x12, waiting for transfers between devices  186 us
    dot_general x12, matrix products, one_block(): within = jnp.einsum('hts,shp->thp', mixing, block_values, precision=HIGHEST)  111 us
    reduce_scatter x1, waiting for transfers between devices, shards(): lax.psum_scatter(state_wgrad, ('dp', 'tensor'), scatter_dimension=0, tile...  100 us
    all_gather x1, blocking collectives, shards(): lax.all_gather(state_weight, ('dp', 'tensor'), axis=0, tiled=True)  72.1 us
    all_gather x1, blocking collectives, shards(): lax.all_gather(conv_weight, ('dp', 'tensor'), axis=1, tiled=True)  66.6 us
    dot_general x16, matrix products, one_block(): jnp.einsum('tn,hpn->thp', block_c, carry_state, precision=HIGHEST)  50.7 us
  transfers between devices with their start and end apart: 9, of which 8 were waited for; matrix products, arithmetic and copies ran while one was open for 5% of the time, Pallas kernels for 0%

commit v1 on v0

v1 whole, which is shorter than its diff:
```python
import functools

import jax
import jax.numpy as jnp
from jax import lax
from jax.experimental import pallas as pl
from jax.experimental.pallas import tpu as pltpu
from jax.sharding import PartitionSpec as P

F32 = jnp.float32
BF16 = jnp.bfloat16
MESH = pl.DeviceIdType.MESH

SPAN = 256
LENGTH = 1024
STEP = 5
LANES = 128
LOG2E = 1.4426950408889634
NORM_EPSILON = 1e-05
FIRST_DECAY = 0.9
SECOND_DECAY = 0.95
ADAM_EPSILON = 1e-08
WEIGHT_DECAY = 0.1
RATE_MATRIX = 0.05
RATE_OUTPUT = 0.04
RATE_CONV = 1.0
RATE_VECTOR = 0.5
RATE_HEADS = 2.0
MIXER_VMEM = 63 * 1024 * 1024


def mm(a, b):
    return lax.dot_general(a, b, (((1,), (0,)), ((), ())), preferred_element_type=F32)


def mm_nt(a, b):
    return lax.dot_general(a, b, (((1,), (1,)), ((), ())), preferred_element_type=F32)


def mm_exact(a, b):
    return lax.dot_general(
        a, b, (((1,), (0,)), ((), ())), preferred_element_type=F32, precision=lax.Precision.HIGHEST
    )


def sigmoid(v):
    return 1.0 / (1.0 + jnp.exp(-v))


def softplus(v):
    return jnp.maximum(v, 0.0) + jnp.log1p(jnp.exp(-jnp.abs(v)))


def split_low(v):
    high = v.astype(BF16)
    return high, (v - high.astype(F32)).astype(BF16)


def head_marks(head_width, channels):
    head = lax.broadcasted_iota(jnp.int32, (LANES, channels), 0)
    channel = lax.broadcasted_iota(jnp.int32, (LANES, channels), 1)
    inside = (channel >= head * head_width) & (channel < (head + 1) * head_width)
    return inside.astype(F32).astype(BF16)


def head_marks_t(head_width, channels):
    head = lax.broadcasted_iota(jnp.int32, (channels, LANES), 1)
    channel = lax.broadcasted_iota(jnp.int32, (channels, LANES), 0)
    inside = (channel >= head * head_width) & (channel < (head + 1) * head_width)
    return inside.astype(F32).astype(BF16)


def spread(v, marks2):
    high, low = split_low(v)
    return mm(jnp.concatenate([high, low], 1), marks2)


def gather_heads(v, marks_t2):
    high, low = split_low(v)
    return mm(jnp.concatenate([high, low], 1), marks_t2)


def causal_ones(lower):
    row = lax.broadcasted_iota(jnp.int32, (SPAN, SPAN), 0)
    col = lax.broadcasted_iota(jnp.int32, (SPAN, SPAN), 1)
    keep = row >= col if lower else row <= col
    return keep.astype(F32)


def lane_masks():
    lane = lax.broadcasted_iota(jnp.int32, (1, LANES), 1)
    first = (lane < LANES // 2).astype(F32)
    return first, 1.0 - first


def sds(shape, dtype):
    return jax.ShapeDtypeStruct(shape, dtype)


def axis_bits(size):
    count = size.bit_length() - 1
    order = list(range(1, count)) + [0]
    other = [order[1], order[0]] + order[2:] if count >= 3 else order
    return order, other


def flipped(index, mask):
    result = index
    bit = 1
    while bit <= mask:
        if mask & bit:
            result = result + bit * (1 - 2 * ((index // bit) % 2))
        bit *= 2
    return result


def gather_weights(
    w_own, st_own, sm_own, w_full, st_full, sm_full, local_sem, z_send, z_recv, send_sem, recv_sem,
    *, dp, tp, cut
):
    me = lax.axis_index("dp")
    tensor = lax.axis_index("tensor")
    rows, width = w_own.shape
    count = dp.bit_length() - 1

    barrier = pltpu.get_barrier_semaphore()
    for b in range(count):
        pl.semaphore_signal(
            barrier, inc=1, device_id=(flipped(me, 1 << b), tensor), device_id_type=MESH
        )
    for k in range(1, tp):
        pl.semaphore_signal(barrier, inc=1, device_id=(me, flipped(tensor, k)), device_id_type=MESH)
    pl.semaphore_wait(barrier, count + tp - 1)

    order, other = axis_bits(dp)
    row_of = lambda mask: pl.multiple_of(flipped(me, mask) * rows, 16)
    left, right = pl.ds(0, cut), pl.ds(cut, width - cut)

    def weight_part(columns):
        def source(mask):
            if mask == 0:
                return w_own.at[:, columns]
            return w_full.at[pl.ds(row_of(mask), rows), columns]

        return source, lambda mask: w_full.at[pl.ds(row_of(mask), rows), columns]

    state_part = (lambda mask: st_full.at[flipped(me, mask)],) * 2
    small_part = (lambda mask: sm_full.at[flipped(me, mask)],) * 2
    kinds = (
        (order, weight_part(left)),
        (other, weight_part(right)),
        (order, state_part),
        (other, small_part),
    )

    def full_mask(bits, packed):
        return sum(1 << bits[j] for j in range(count) if packed >> j & 1)

    def move(kind, packed, j):
        bits, (source, target) = kinds[kind]
        mask = full_mask(bits, packed)
        slot = packed | (1 << j)
        return pltpu.make_async_remote_copy(
            src_ref=source(mask),
            dst_ref=target(mask),
            send_sem=send_sem.at[kind, slot],
            recv_sem=recv_sem.at[kind, slot],
            device_id=(flipped(me, 1 << bits[j]), tensor),
            device_id_type=MESH,
        )

    started = []

    def start(kind, packed, j):
        copy = move(kind, packed, j)
        copy.start()
        started.append(copy)

    zs = []
    for k in range(1, tp):
        for which, (own, full) in enumerate(((st_own, st_full), (sm_own, sm_full))):
            copy = pltpu.make_async_remote_copy(
                src_ref=own,
                dst_ref=full.at[me, tensor],
                send_sem=z_send.at[which, k],
                recv_sem=z_recv.at[which, k],
                device_id=(me, flipped(tensor, k)),
                device_id_type=MESH,
            )
            copy.start()
            zs.append(copy)
    for j in range(count):
        for kind in (0, 1):
            start(kind, 0, j)
    locals_ = [
        pltpu.make_async_copy(w_own, w_full.at[pl.ds(row_of(0), rows)], local_sem.at[0]),
        pltpu.make_async_copy(st_own, st_full.at[me, tensor], local_sem.at[1]),
        pltpu.make_async_copy(sm_own, sm_full.at[me, tensor], local_sem.at[2]),
    ]
    for copy in locals_:
        copy.start()
    for copy in locals_:
        copy.wait()
    for copy in zs:
        copy.wait()
    for j in range(count):
        for kind in (3, 2):
            start(kind, 0, j)
    for packed in range(1, dp):
        top = packed.bit_length() - 1
        for kind in (0, 1, 3, 2):
            move(kind, packed & ~(1 << top), top).wait_recv()
            for j in range(top + 1, count):
                start(kind, packed, j)
    for copy in started:
        copy.wait_send()


def run_gather(w_own, st_own, sm_own, dp, tp):
    rows, width = w_own.shape
    cut = width // 2 // LANES * LANES
    hbm = pl.BlockSpec(memory_space=pl.ANY)
    return pl.pallas_call(
        functools.partial(gather_weights, dp=dp, tp=tp, cut=cut),
        in_specs=[hbm] * 3,
        out_specs=(hbm,) * 3,
        out_shape=(
            sds((dp * rows, width), BF16),
            sds((dp, tp) + st_own.shape, BF16),
            sds((dp, tp) + sm_own.shape, F32),
        ),
        scratch_shapes=[
            pltpu.SemaphoreType.DMA((3,)),
            pltpu.SemaphoreType.DMA((2, tp)),
            pltpu.SemaphoreType.DMA((2, tp)),
            pltpu.SemaphoreType.DMA((4, dp)),
            pltpu.SemaphoreType.DMA((4, dp)),
        ],
        compiler_params=pltpu.CompilerParams(collective_id=1, has_side_effects=True),
        name="gather_weights",
    )(w_own, st_own, sm_own)


def add_low(a, b):
    return (a.astype(F32) + b.astype(F32)).astype(BF16)


HALF = SPAN // 2


def forward_step(f, x, c, w_v, ws_v, pv, saved, state_v, ext, stage, stats, sizes):
    inner, head_width, heads = sizes
    cin_s, pre_s, gate_s, y_s, sp_s, state_s = saved
    states = ws_v.shape[1] // 2
    conv = inner + 2 * states

    x = x[...].astype(F32)
    inv = lax.rsqrt(jnp.mean(x * x, axis=1, keepdims=True) + NORM_EPSILON)
    normed = (x * inv * pv[0:1, :]).astype(BF16)

    step_in = mm(normed, w_v[:, 2 * inner : 2 * inner + LANES])
    sp_s[f] = step_in
    ext[8:, 0:inner] = mm(normed, w_v[:, inner : 2 * inner])
    ext[8:, inner:conv] = mm(normed, ws_v[...])
    gate = mm(normed, w_v[:, 0:inner]).astype(BF16)
    gate_s[f] = gate
    gate = gate.astype(F32)
    cin_s[f] = ext[8:, :].astype(BF16)
    pre = pv[6:7, 0:conv]
    for tap in range(4):
        pre = pre + pv[2 + tap : 3 + tap, 0:conv] * ext[5 + tap : 5 + tap + SPAN, :]
    ext[0:8, :] = ext[SPAN : SPAN + 8, :]
    pre = pre.astype(BF16)
    pre_s[f] = pre
    pre = pre.astype(F32)
    act = pre * sigmoid(pre)

    rate = pv[7:8, 0:LANES]
    dt = softplus(step_in + pv[7:8, LANES : 2 * LANES])
    total = mm_exact(causal_ones(True), dt * rate)
    total2 = total * LOG2E
    total2_t = jnp.transpose(total2)
    marks = head_marks(head_width, inner)
    marks2 = jnp.concatenate([marks, marks], 0)
    end = total[SPAN - 1 : SPAN, :]
    xc = act[:, 0:inner]
    bmat = act[:, inner : inner + states].astype(BF16)
    cmat = act[:, inner + states :].astype(BF16)
    xd = (xc * spread(dt, marks2)).astype(BF16)
    weighted = (xd.astype(F32) * spread(jnp.exp(end - total), marks2)).astype(BF16)

    state = state_v[...]
    state_low = state.astype(BF16)
    state_s[f] = state_low
    carried = spread(jnp.exp(total), marks2) * mm(cmat, state_low)
    keep = spread(jnp.broadcast_to(jnp.exp(end), (8, LANES)), marks2)[0:1, :]
    state_v[...] = keep * state + mm(jnp.transpose(bmat), weighted)

    inter = mm_nt(cmat, bmat) * causal_ones(True)
    first, second = lane_masks()
    skip = pv[1:2, inner : 2 * inner]
    parts = []
    for pair in range(heads // 2):
        lanes = slice(pair * LANES, (pair + 1) * LANES)
        xp = xd[:, lanes].astype(F32)
        within = None
        for side, mask in ((0, first), (1, second)):
            h = 2 * pair + side
            gap = jnp.minimum(total2[:, h : h + 1] - total2_t[h : h + 1, :], 0.0)
            mixing = (jnp.exp2(gap) * inter).astype(BF16)
            term = mm(mixing, (xp * mask).astype(BF16))
            within = term if within is None else within + term
        parts.append(within)
    y = jnp.concatenate(parts, 1) + carried
    y_s[f] = y
    y = y + skip * xc
    gated = y * gate * sigmoid(gate)
    squares = jnp.sum(gated * gated, axis=1, keepdims=True)
    lowered = (gated * pv[1:2, 0:inner]).astype(BF16)
    out = mm_nt(lowered, w_v[:, 2 * inner + LANES :])
    stage[...] = out.astype(BF16).reshape(stage.shape)
    dots = jnp.sum(c[...].astype(F32) * out, axis=1, keepdims=True)
    lane = lax.broadcasted_iota(jnp.int32, (SPAN, LANES), 1)
    both = jnp.where(lane == 0, squares, jnp.where(lane == 1, dots, 0.0))
    stats[...] = jnp.transpose(both)[0:8, :]


def backward_step(
    f, x, c, w_v, ws_v, pv, totals, saved, dst_v, dext, small, grads, lowered_v, turned, put, stage, sizes, norm_width
):
    inner, head_width, heads = sizes
    cin_s, pre_s, gate_s, y_s, sp_s, state_s = saved
    states = ws_v.shape[1] // 2
    conv = inner + 2 * states
    put_grads, put_lowered, put_branch, put_normed = put

    sums = jnp.transpose(jnp.concatenate([totals] * (LANES // 8), 0))
    scale = lax.rsqrt(sums[:, 0:1] / norm_width + NORM_EPSILON)
    bg = (scale * c[...].astype(F32)).astype(BF16)
    squares_grad = (-0.5 / norm_width) * sums[:, 1:2] * scale * scale * scale
    low_grad = mm(bg, w_v[:, 2 * inner + LANES :])

    pre = pre_s[f].astype(F32)
    sig_pre = sigmoid(pre)
    act = pre * sig_pre
    xc = act[:, 0:inner]
    bmat = act[:, inner : inner + states].astype(BF16)
    cmat = act[:, inner + states :].astype(BF16)

    skip = pv[1:2, inner : 2 * inner]
    gate = gate_s[f].astype(F32)
    sig = sigmoid(gate)
    y_scan = y_s[f]
    y = y_scan + skip * xc
    silu_gate = gate * sig
    gated = y * silu_gate
    gain = pv[1:2, 0:inner]
    lowered_v[...] = (gated * gain).astype(BF16)
    put_lowered.start()
    gated_grad = low_grad * gain + 2.0 * gated * squares_grad
    small[1:2, 0:inner] += jnp.sum(low_grad * gated, axis=0, keepdims=True)
    y_grad = gated_grad * silu_gate
    grads[:, 0:inner] = (gated_grad * y * sig * (1.0 + gate * (1.0 - sig))).astype(BF16)
    small[1:2, inner : 2 * inner] += jnp.sum(y_grad * xc, axis=0, keepdims=True)

    turned[...] = jnp.transpose(bg)
    put_branch.start()

    rate = pv[7:8, 0:LANES]
    step_pre = sp_s[f] + pv[7:8, LANES : 2 * LANES]
    dt = softplus(step_pre)
    total = mm_exact(causal_ones(True), dt * rate)
    total2 = total * LOG2E
    total2_t = jnp.transpose(total2)
    marks = head_marks(head_width, inner)
    marks2 = jnp.concatenate([marks, marks], 0)
    marks_t = head_marks_t(head_width, inner)
    marks_t2 = jnp.concatenate([marks_t, marks_t], 0)
    end = total[SPAN - 1 : SPAN, :]
    dt_wide = spread(dt, marks2)
    xd = (xc * dt_wide).astype(BF16)
    xd_wide = xd.astype(F32)
    end_wide = spread(jnp.exp(end - total), marks2)

    yb = y_grad.astype(BF16)
    yb_wide = yb.astype(F32)
    state_low = state_s[f]
    dst = dst_v[...]
    dst_low = dst.astype(BF16)
    carried_grad = (yb_wide * spread(jnp.exp(total), marks2)).astype(BF16)
    c_grad = mm_nt(carried_grad, state_low)
    b_state = mm(bmat, dst_low) * end_wide
    b_grad = mm_nt((xd_wide * end_wide).astype(BF16), dst_low)
    keep = spread(jnp.broadcast_to(jnp.exp(end), (8, LANES)), marks2)[0:1, :]
    end_row = jnp.sum(xd_wide * b_state, axis=0, keepdims=True) + keep * jnp.sum(
        dst * state_low.astype(F32), axis=0, keepdims=True
    )
    dst_v[...] = keep * dst + mm(jnp.transpose(cmat), carried_grad)

    causal = causal_ones(True)
    inter = mm_nt(cmat, bmat) * causal
    first, second = lane_masks()
    inter_grad = jnp.zeros((SPAN, SPAN), F32)
    yb_t = jnp.transpose(yb)
    parts = []
    for pair in range(heads // 2):
        lanes = slice(pair * LANES, (pair + 1) * LANES)
        xp = xd[:, lanes]
        yp = yb_wide[:, lanes]
        for side, mask in ((0, first), (1, second)):
            h = 2 * pair + side
            gap = jnp.minimum(total2[:, h : h + 1] - total2_t[h : h + 1, :], 0.0)
            fade = jnp.exp2(gap)
            mixing = (fade * inter).astype(BF16)
            inter_grad = inter_grad + mm_nt((yp * mask).astype(BF16), xp) * fade
            parts.append(mm(yb_t[h * head_width : (h + 1) * head_width, :], mixing))
    xd_grad = jnp.transpose(jnp.concatenate(parts, 0)) + b_state
    inter_low = (inter_grad * causal).astype(BF16)
    c_grad = c_grad + mm(inter_low, bmat)
    b_grad = b_grad + mm(jnp.transpose(inter_low), cmat)

    rows = gather_heads(yb_wide * y_scan - xd_wide * xd_grad, marks_t2)
    end_sum = gather_heads(jnp.broadcast_to(end_row, (8, inner)), marks_t2)[0:1, :]
    decay_grad = mm_exact(causal_ones(False), rows) + end_sum
    dt_grad = decay_grad * rate + gather_heads(xc * xd_grad, marks_t2)
    small[7:8, 0:LANES] += jnp.sum(decay_grad * dt, axis=0, keepdims=True) * rate
    step_grad = dt_grad * sigmoid(step_pre)
    small[7:8, LANES : 2 * LANES] += jnp.sum(step_grad, axis=0, keepdims=True)
    grads[:, conv + inner :] = step_grad.astype(BF16)

    x_grad = xd_grad * dt_wide + skip * y_grad
    act_grad = jnp.concatenate([x_grad, b_grad, c_grad], 1)
    pre = pre_s[f].astype(F32)
    sig_pre = sigmoid(pre)
    pre_grad = act_grad * sig_pre * (1.0 + pre * (1.0 - sig_pre))
    dext[0:SPAN, :] = pre_grad
    small[6:7, 0:conv] += jnp.sum(pre_grad, axis=0, keepdims=True)
    conv_in = cin_s[f].astype(F32)
    conv_grad = None
    for tap in range(4):
        shifted = dext[3 - tap : 3 - tap + SPAN, :]
        term = pv[2 + tap : 3 + tap, 0:conv] * shifted
        conv_grad = term if conv_grad is None else conv_grad + term
        small[2 + tap : 3 + tap, 0:conv] += jnp.sum(conv_in * shifted, axis=0, keepdims=True)
    dext[SPAN:, :] = dext[0:8, :]
    grads[:, inner : inner + conv] = conv_grad.astype(BF16)

    normed_grad = mm_nt(grads[:, 0 : 2 * inner], w_v[:, 0 : 2 * inner])
    normed_grad = normed_grad + mm_nt(grads[:, 2 * inner : inner + conv], ws_v[...])
    normed_grad = normed_grad + mm_nt(
        grads[:, inner + conv :], w_v[:, 2 * inner : 2 * inner + LANES]
    )
    x = x[...].astype(F32)
    inv = lax.rsqrt(jnp.mean(x * x, axis=1, keepdims=True) + NORM_EPSILON)
    scaled_x = x * inv
    small[0:1, :] += jnp.sum(normed_grad * scaled_x, axis=0, keepdims=True)
    scaled = normed_grad * pv[0:1, :]
    inner_mean = jnp.mean(x * scaled, axis=1, keepdims=True)
    part = inv * scaled - x * (inv * inv * inv * inner_mean)
    stage[...] = part.astype(BF16).reshape(stage.shape)

    put_branch.wait()
    turned[...] = jnp.transpose((scaled_x * pv[0:1, :]).astype(BF16))
    put_normed.start()
    put_grads.start()


def mixer(
    x_hbm,
    c_hbm,
    w_hbm,
    ws_hbm,
    pv,
    edge,
    across,
    mine,
    rs1,
    rs2,
    grads_hbm,
    lowered_hbm,
    branch_hbm,
    normed_hbm,
    own,
    vectors,
    head_sums,
    totals,
    w_v,
    ws_v,
    xbuf,
    cbuf,
    cin_s,
    pre_s,
    gate_s,
    y_s,
    sp_s,
    state_s,
    state_v,
    dst_v,
    ext,
    wgrad,
    tiles,
    small,
    grads,
    lowered_v,
    turned,
    stage,
    landed,
    mine_v,
    pair,
    total_v,
    rsv,
    stat_own,
    stat_in,
    small1,
    small2,
    small3,
    w_sem,
    load_sem,
    edge_send,
    edge_recv,
    across_send,
    across_recv,
    keep_sem,
    mine_sem,
    pump_sem,
    stat_send,
    stat_recv,
    rs1_send,
    rs1_recv,
    rs2_send,
    rs2_recv,
    rs_sem,
    put_sem,
    tile_sem,
    sm_send,
    sm_recv,
    *,
    dp,
    tp,
    sizes,
    norm_width,
):
    me = lax.axis_index("dp")
    z = lax.axis_index("tensor")
    inner, head_width, heads = sizes
    tokens, depth = x_hbm.shape
    blocks = tokens // SPAN
    per = LENGTH // SPAN
    sequences = blocks // per
    cycle = 2 * per
    pieces = 2 * blocks
    half = dp // 2
    rows = depth // dp
    conv = inner + ws_hbm.shape[1]
    wide = inner + conv + LANES
    saved = (cin_s, pre_s, gate_s, y_s, sp_s, state_s)
    parity = lax.rem(me, 2)
    chip = me // 2
    sibling = me + 1 - 2 * parity
    is_middle = (z == 1) | (z == 2)
    is_end = (z == 0) | (z == 3)
    edge_peer = flipped(z, 1)
    across_peer = 3 - z

    barrier = pltpu.get_barrier_semaphore()
    greet = [(sibling, z)]
    greet += [(2 * lax.rem(chip + k, half) + parity, z) for k in range(1, half)]
    greet += [(me, flipped(z, k)) for k in range(1, tp)]
    for device in greet:
        pl.semaphore_signal(barrier, inc=1, device_id=device, device_id_type=MESH)

    loads_w = [
        pltpu.make_async_copy(w_hbm, w_v, w_sem.at[0]),
        pltpu.make_async_copy(ws_hbm, ws_v, w_sem.at[1]),
    ]
    for copy in loads_w:
        copy.start()

    def block_of(n):
        s, r = n // cycle, lax.rem(n, cycle)
        back = r // per
        pos = lax.rem(r, per)
        return per * s + (1 - back) * pos + back * (per - 1 - pos)

    def slot_of(n):
        return blocks * (lax.rem(n, cycle) // per) + block_of(n)

    def loads(n):
        slot = lax.rem(n, 2)
        at = pl.multiple_of(block_of(n) * SPAN, SPAN)
        return [
            pltpu.make_async_copy(x_hbm.at[pl.ds(at, SPAN)], xbuf.at[slot], load_sem.at[0, slot]),
            pltpu.make_async_copy(c_hbm.at[pl.ds(at, SPAN)], cbuf.at[slot], load_sem.at[1, slot]),
        ]

    def next_block(n):
        for copy in loads(n):
            copy.wait()

        @pl.when(n + 1 < pieces)
        def _():
            for copy in loads(n + 1):
                copy.start()

    def edge_copy(n, h, source):
        slot = slot_of(n)
        return pltpu.make_async_remote_copy(
            src_ref=source,
            dst_ref=edge.at[slot, h],
            send_sem=edge_send.at[slot, h],
            recv_sem=edge_recv.at[slot, h],
            device_id=(me, edge_peer),
            device_id_type=MESH,
        )

    def inward(n, h):
        return edge_copy(n, h, mine.at[slot_of(n), h])

    def outward(n, h):
        return edge_copy(n, h, total_v.at[lax.rem(n, 2), h])

    def kept(n, h):
        slot = slot_of(n)
        return pltpu.make_async_copy(total_v.at[lax.rem(n, 2), h], edge.at[slot, h], keep_sem.at[slot, h])

    def across_copy(n, h):
        slot = slot_of(n)
        return pltpu.make_async_remote_copy(
            src_ref=pair.at[lax.rem(n, 2), h],
            dst_ref=across.at[slot, h],
            send_sem=across_send.at[slot, h],
            recv_sem=across_recv.at[slot, h],
            device_id=(me, across_peer),
            device_id_type=MESH,
        )

    def landing(source, n, h):
        return pltpu.make_async_copy(source.at[slot_of(n), h], landed.at[h], pump_sem.at[h])

    def mine_load(n):
        return pltpu.make_async_copy(mine.at[slot_of(n)], mine_v, pump_sem.at[2])

    def store_piece(n):
        return pltpu.make_async_copy(stage, mine.at[slot_of(n)], mine_sem.at[0])

    def in_groups(apart, arrived, load, place, send):
        for group in ((0,), (1,)) if apart else ((0, 1),):
            for h in group:
                arrived(h)
            for h in group:
                load(h).start()
            for h in group:
                load(h).wait()
            for h in group:
                place(h)
                send(h)

    def combine(n, apart=False):
        mine_load(n).start()

        @pl.when(n >= 2)
        def _():
            for h in (0, 1):
                across_copy(n - 2, h).wait_send()

        mine_load(n).wait()
        slot = lax.rem(n, 2)

        def place(h):
            pair[slot, h] = add_low(mine_v[h], landed[h])

        in_groups(
            apart,
            lambda h: inward(n, h).wait_recv(),
            lambda h: landing(edge, n, h),
            place,
            lambda h: across_copy(n, h).start(),
        )

    def finish(n, apart=False):
        @pl.when(n >= 2)
        def _():
            for h in (0, 1):
                outward(n - 2, h).wait_send()
                kept(n - 2, h).wait()

        slot = lax.rem(n, 2)

        def place(h):
            total_v[slot, h] = add_low(pair[slot, h], landed[h])

        def send(h):
            outward(n, h).start()
            kept(n, h).start()

        in_groups(
            apart,
            lambda h: across_copy(n, h).wait_recv(),
            lambda h: landing(across, n, h),
            place,
            send,
        )

    def combined(n):
        return jnp.maximum(2 * n - 3, 0) // 3

    def sent(n):
        paced = combined(n) + 2 + lax.rem(n, cycle) // per
        return jnp.where(n == pieces - 1, pieces, jnp.where(n < 0, 0, jnp.minimum(n + 1, paced)))

    def pump(n):
        @pl.when(is_end)
        def _():
            @pl.loop(sent(n - 1), sent(n))
            def _(k):
                for h in (0, 1):
                    inward(k, h).start()

        @pl.when(is_middle & (combined(n - 2) > combined(n - 3)))
        def _():
            finish(combined(n - 2) - 1)

        @pl.when(is_middle & (combined(n) > combined(n - 1)))
        def _():
            combine(combined(n) - 1)

    def advance(n, apart=False):
        @pl.when(is_middle)
        def _():
            combine(n, apart)
            finish(n - 1, apart)

    def puts(b, which):
        pairs = (
            (grads, grads_hbm),
            (lowered_v, lowered_hbm),
            (turned, branch_hbm),
            (turned, normed_hbm),
        )
        return [
            pltpu.make_async_copy(pairs[k][0], pairs[k][1].at[b], put_sem.at[k]) for k in which
        ]

    def stat_copy(s, k):
        return pltpu.make_async_remote_copy(
            src_ref=stat_own.at[s],
            dst_ref=stat_in.at[s, k - 1],
            send_sem=stat_send.at[s, k - 1],
            recv_sem=stat_recv.at[s, k - 1],
            device_id=(me, flipped(z, k)),
            device_id_type=MESH,
        )

    for copy in loads(0):
        copy.start()
    small[...] = jnp.zeros_like(small)
    pl.semaphore_wait(barrier, len(greet))
    for copy in loads_w:
        copy.wait()

    @pl.loop(0, sequences)
    def _(s):
        first_n = s * cycle
        ext[0:8, :] = jnp.zeros((8, conv), F32)
        state_v[...] = jnp.zeros_like(state_v)

        @pl.loop(0, per)
        def _(f):
            n = first_n + f
            next_block(n)
            slot = lax.rem(n, 2)
            forward_step(
                f,
                xbuf.at[slot],
                cbuf.at[slot],
                w_v,
                ws_v,
                pv,
                saved,
                state_v,
                ext,
                stage,
                stat_own.at[s, f],
                sizes,
            )

            store_piece(n).start()

            @pl.when(f == per - 1)
            def _():
                for k in range(1, tp):
                    stat_copy(s, k).start()

            store_piece(n).wait()
            pump(n)

        for k in range(1, tp):
            stat_copy(s, k).wait()
        ext[SPAN:, :] = jnp.zeros((8, conv), F32)
        dst_v[...] = jnp.zeros_like(dst_v)
        totals[s] = (stat_own[s] + stat_in[s, 0]) + (stat_in[s, 1] + stat_in[s, 2])

        @pl.loop(0, per)
        def _(j):
            n = first_n + per + j
            f = per - 1 - j
            b = per * s + f
            next_block(n)

            @pl.when(b != per - 1)
            def _():
                for copy in puts(b, (0, 1, 3)):
                    copy.wait()

            slot = lax.rem(n, 2)
            backward_step(
                f,
                xbuf.at[slot],
                cbuf.at[slot],
                w_v,
                ws_v,
                pv,
                totals[s, f],
                saved,
                dst_v,
                ext,
                small,
                grads,
                lowered_v,
                turned,
                puts(b, range(4)),
                stage,
                sizes,
                norm_width,
            )
            store_piece(n).start()
            store_piece(n).wait()
            pump(n)

    def to_sibling(q):
        at = pl.multiple_of((2 * q + 1 - parity) * rows, 16)
        return pltpu.make_async_remote_copy(
            src_ref=wgrad.at[pl.ds(at, rows)],
            dst_ref=rs1.at[q],
            send_sem=rs1_send.at[q],
            recv_sem=rs1_recv.at[q],
            device_id=(sibling, z),
            device_id_type=MESH,
        )

    def to_owner(k):
        q = lax.rem(chip + k, half)
        at = pl.multiple_of((2 * q + parity) * rows, 16)
        return pltpu.make_async_remote_copy(
            src_ref=wgrad.at[pl.ds(at, rows)],
            dst_ref=rs2.at[chip],
            send_sem=rs2_send.at[k],
            recv_sem=rs2_recv.at[k],
            device_id=(2 * q + parity, z),
            device_id_type=MESH,
        )

    def small_copy(source, target, index, device):
        return pltpu.make_async_remote_copy(
            src_ref=source,
            dst_ref=target,
            send_sem=sm_send.at[index],
            recv_sem=sm_recv.at[index],
            device_id=device,
            device_id_type=MESH,
        )

    def fetch(source):
        copy = pltpu.make_async_copy(source, rsv, rs_sem.at[0])
        copy.start()
        copy.wait()
        return rsv[...].astype(F32)

    def left_operand(source):
        return [
            pltpu.make_async_copy(source.at[b], w_v.at[:, pl.ds(b * SPAN, SPAN)], tile_sem.at[2 + b])
            for b in range(blocks)
        ]

    def tile_load(source, at, size, slot):
        return pltpu.make_async_copy(
            source.at[:, :, pl.ds(at, size)], tiles.at[slot, :, :, pl.ds(0, size)], tile_sem.at[slot]
        )

    def products(source, width, place):
        whole = width // 256

        @pl.loop(0, whole)
        def _(t):
            slot = lax.rem(t, 2)
            at = pl.multiple_of(t * 256, 256)
            tile_load(source, at, 256, slot).wait()

            @pl.when(t + 1 < whole)
            def _():
                tile_load(source, pl.multiple_of(at + 256, 256), 256, 1 - slot).start()

            right = tiles[slot].reshape(tokens, 256)
            wgrad[:, pl.ds(pl.multiple_of(place + at, 128), 256)] = mm(
                w_v[:, 0:tokens], right
            ).astype(BF16)

    for copy in puts(per * (sequences - 1), (0, 1, 3)):
        copy.wait()
    for copy in left_operand(normed_hbm):
        copy.start()
    tile_load(grads_hbm, 0, 256, 0).start()
    for copy in left_operand(normed_hbm):
        copy.wait()
    products(grads_hbm, wide, 0)
    rest = wide % 256
    last = tile_load(grads_hbm, wide - rest, rest, 0)
    last.start()
    last.wait()
    wgrad[:, wide - rest : wide] = mm(
        w_v[:, 0:tokens], tiles[0].reshape(tokens, 256)[:, 0:rest]
    ).astype(BF16)
    for copy in left_operand(branch_hbm):
        copy.start()
    tile_load(lowered_hbm, 0, 256, 0).start()

    head = (2 * (pieces - 1) - 3) // 3

    @pl.when(is_middle)
    def _():
        for n in range((2 * (pieces - 3) - 3) // 3, head - 1):
            finish(n)

    advance(head)
    for copy in left_operand(branch_hbm):
        copy.wait()
    products(lowered_hbm, inner, wide)

    @pl.loop(0, half)
    def _(q):
        to_sibling(q).start()

    first_small = small_copy(small, small1, 0, (sibling, z))
    first_small.start()
    spread_over = pieces - 1 - head
    early = head + 1 + max(spread_over // 3, 0)
    for n in range(head + 1, early):
        advance(n)
    first_small.wait()
    small2[chip] = small[...] + small1[...]
    second_small = [
        small_copy(
            small2.at[chip], small2.at[chip], k, (2 * lax.rem(chip + k, half) + parity, z)
        )
        for k in range(1, half)
    ]
    for copy in second_small:
        copy.start()

    @pl.loop(1, half)
    def _(k):
        q = lax.rem(chip + k, half)
        to_sibling(q).wait_recv()
        at = pl.multiple_of((2 * q + parity) * rows, 16)
        wgrad[pl.ds(at, rows), :] = (
            wgrad[pl.ds(at, rows), :].astype(F32) + fetch(rs1.at[q])
        ).astype(BF16)
        to_owner(k).start()

    late = max(early, pieces - 2)
    for n in range(early, late):
        advance(n)
    to_sibling(chip).wait_recv()
    own[...] = wgrad[pl.ds(pl.multiple_of(me * rows, 16), rows), :].astype(F32) + fetch(
        rs1.at[chip]
    )
    for copy in second_small:
        copy.wait()
    total = small2[0]
    for q in range(1, half):
        total = total + small2[q]
    small3[z] = total
    third_small = [
        small_copy(small3.at[z], small3.at[z], half + k, (me, flipped(z, k)))
        for k in range(1, tp)
    ]
    for copy in third_small:
        copy.start()
    for n in range(late, pieces - 1):
        advance(n, True)

    @pl.loop(1, half)
    def _(k):
        to_owner(k).wait_recv()
        own[...] += fetch(rs2.at[lax.rem(chip + half - k, half)])

    advance(pieces - 1, True)
    for copy in third_small:
        copy.wait()
    vectors[...] = jnp.zeros_like(vectors)
    both = conv - inner
    shared = small3[0, 2:7, inner:conv]
    before = small3[0, 0:1, :]
    for k in range(1, tp):
        shared = shared + small3[k, 2:7, inner:conv]
        before = before + small3[k, 0:1, :]
    for k in range(tp):
        vectors[0:5, k * inner : (k + 1) * inner] = small3[k, 2:7, 0:inner]
        vectors[5:6, depth + k * inner : depth + (k + 1) * inner] = small3[k, 1:2, 0:inner]
        head_sums[k, 0:1, :] = small3[k, 7:8, 0:LANES]
        head_sums[k, 1:2, :] = small3[k, 7:8, LANES : 2 * LANES]
        marks_t = head_marks_t(head_width, inner)
        skips = gather_heads(
            jnp.broadcast_to(small3[k, 1:2, inner : 2 * inner], (8, inner)),
            jnp.concatenate([marks_t, marks_t], 0),
        )
        head_sums[k, 2:8, :] = skips[2:8, :]
    vectors[0:5, tp * inner : tp * inner + both] = shared
    vectors[5:6, 0:depth] = before

    @pl.when(is_middle)
    def _():
        finish(pieces - 1, True)

    @pl.loop(0, half)
    def _(q):
        to_sibling(q).wait_send()

    @pl.loop(1, half)
    def _(k):
        to_owner(k).wait_send()

    @pl.when(is_middle)
    def _():
        for n in (pieces - 2, pieces - 1):
            for h in (0, 1):
                across_copy(n, h).wait_send()
                outward(n, h).wait_send()
                kept(n, h).wait()

    @pl.when(is_end)
    def _():
        @pl.loop(0, pieces)
        def _(n):
            for h in (0, 1):
                inward(n, h).wait_send()
                outward(n, h).wait_recv()


def finalize(x_ref, c_ref, out_ref, in_ref, totals_ref, block_ref, grad_ref, *, norm_width):
    sums = jnp.transpose(jnp.concatenate([totals_ref[0, 0]] * (LANES // 8), 0))
    scale = lax.rsqrt(sums[:, 0:1] / norm_width + NORM_EPSILON)
    shape = x_ref.shape
    branch = out_ref[0].reshape(shape).astype(F32)
    block_ref[...] = (x_ref[...].astype(F32) + scale * branch).astype(BF16)
    grad_ref[...] = in_ref[0].reshape(shape).astype(F32) + c_ref[...].astype(F32)


def run_finalize(x, c, sums, totals, norm_width):
    tokens, depth = x.shape
    blocks = tokens // SPAN
    per = LENGTH // SPAN
    rows = pl.BlockSpec((SPAN, depth), lambda b: (b, 0))
    return pl.pallas_call(
        functools.partial(finalize, norm_width=norm_width),
        grid=(blocks,),
        in_specs=[
            rows,
            rows,
            pl.BlockSpec((1, 2, HALF, depth), lambda b: (b, 0, 0, 0)),
            pl.BlockSpec((1, 2, HALF, depth), lambda b: (blocks + b, 0, 0, 0)),
            pl.BlockSpec((1, 1, 8, SPAN), lambda b: (b // per, b % per, 0, 0)),
        ],
        out_specs=(rows, rows),
        out_shape=(sds((tokens, depth), BF16), sds((tokens, depth), F32)),
        compiler_params=pltpu.CompilerParams(vmem_limit_bytes=32 * 1024 * 1024),
        cost_estimate=pl.CostEstimate(
            flops=6 * tokens * depth, bytes_accessed=14 * tokens * depth, transcendentals=0
        ),
        name="finalize",
    )(x, c, sums, sums, totals)


def run_mixer(x, c, w, ws, pv, dp, tp, sizes, norm_width):
    inner, head_width, heads = sizes
    tokens, depth = x.shape
    conv_states = ws.shape[1]
    conv = inner + conv_states
    states = conv_states // 2
    wide = inner + conv + LANES
    width = w.shape[1]
    blocks = tokens // SPAN
    per = LENGTH // SPAN
    sequences = blocks // per
    pieces = 2 * blocks
    half = dp // 2
    rows = depth // dp
    hbm = pl.BlockSpec(memory_space=pl.ANY)
    vmem = pl.BlockSpec(memory_space=pltpu.VMEM)
    dma = pltpu.SemaphoreType.DMA
    piece = (2, HALF, depth)
    rows_of_x = (SPAN, depth)
    flops = tokens * (6 * depth * (2 * inner + conv) + 6 * depth * inner + 80 * heads * SPAN * 64)
    return pl.pallas_call(
        functools.partial(mixer, dp=dp, tp=tp, sizes=sizes, norm_width=norm_width),
        in_specs=[hbm] * 4 + [vmem],
        out_specs=(hbm,) * 9 + (vmem,) * 4,
        out_shape=(
            sds((pieces,) + piece, BF16),
            sds((pieces,) + piece, BF16),
            sds((pieces,) + piece, BF16),
            sds((half, rows, wide + inner), BF16),
            sds((half, rows, wide + inner), BF16),
            sds((blocks, SPAN, wide), BF16),
            sds((blocks, SPAN, inner), BF16),
            sds((blocks, depth, SPAN), BF16),
            sds((blocks, depth, SPAN), BF16),
            sds((rows, wide + inner), F32),
            sds((8, tp * inner + depth), F32),
            sds((tp, 8, LANES), F32),
            sds((sequences, per, 8, SPAN), F32),
        ),
        scratch_shapes=[
            pltpu.VMEM((depth, width), BF16),
            pltpu.VMEM((depth, conv_states), BF16),
            pltpu.VMEM((2,) + rows_of_x, BF16),
            pltpu.VMEM((2,) + rows_of_x, BF16),
            pltpu.VMEM((per, SPAN, conv), BF16),
            pltpu.VMEM((per, SPAN, conv), BF16),
            pltpu.VMEM((per, SPAN, inner), BF16),
            pltpu.VMEM((per, SPAN, inner), F32),
            pltpu.VMEM((per, SPAN, LANES), F32),
            pltpu.VMEM((per, states, inner), BF16),
            pltpu.VMEM((states, inner), F32),
            pltpu.VMEM((states, inner), F32),
            pltpu.VMEM((SPAN + 8, conv), F32),
            pltpu.VMEM((depth, wide + inner), BF16),
            pltpu.VMEM((2, blocks, SPAN, 256), BF16),
            pltpu.VMEM((8, depth), F32),
            pltpu.VMEM((SPAN, wide), BF16),
            pltpu.VMEM((SPAN, inner), BF16),
            pltpu.VMEM((depth, SPAN), BF16),
            pltpu.VMEM(piece, BF16),
            pltpu.VMEM(piece, BF16),
            pltpu.VMEM(piece, BF16),
            pltpu.VMEM((2,) + piece, BF16),
            pltpu.VMEM((2,) + piece, BF16),
            pltpu.VMEM((rows, wide + inner), BF16),
            pltpu.VMEM((sequences, per, 8, SPAN), F32),
            pltpu.VMEM((sequences, tp - 1, per, 8, SPAN), F32),
            pltpu.VMEM((8, depth), F32),
            pltpu.VMEM((half, 8, depth), F32),
            pltpu.VMEM((tp, 8, depth), F32),
            dma((2,)),
            dma((2, 2)),
            dma((pieces, 2)),
            dma((pieces, 2)),
            dma((pieces, 2)),
            dma((pieces, 2)),
            dma((pieces, 2)),
            dma((1,)),
            dma((3,)),
            dma((sequences, tp - 1)),
            dma((sequences, tp - 1)),
            dma((half,)),
            dma((half,)),
            dma((half,)),
            dma((half,)),
            dma((1,)),
            dma((4,)),
            dma((2 + blocks,)),
            dma((half + tp,)),
            dma((half + tp,)),
        ],
        compiler_params=pltpu.CompilerParams(
            collective_id=2, has_side_effects=True, vmem_limit_bytes=MIXER_VMEM
        ),
        cost_estimate=pl.CostEstimate(flops=flops, bytes_accessed=60_000_000, transcendentals=0),
        name="mixer",
    )(x, c, w, ws, pv)


def adamw_update(weight, gradient, moment, square, step_rate, decay_rate):
    moment = FIRST_DECAY * moment + (1.0 - FIRST_DECAY) * gradient
    square = SECOND_DECAY * square + (1.0 - SECOND_DECAY) * gradient * gradient
    first_fix = 1.0 - FIRST_DECAY**STEP
    second_fix = 1.0 - SECOND_DECAY**STEP
    update = moment / first_fix / (jnp.sqrt(square / second_fix) + ADAM_EPSILON)
    return (weight - step_rate * (update + decay_rate * weight), moment, square)


def swap(values, mask, tp):
    return lax.ppermute(values, "tensor", [(i, i ^ mask) for i in range(tp)])


def pad_to(values, size):
    return jnp.pad(values, [(0, 0)] * (values.ndim - 1) + [(0, size - values.shape[-1])])


def shards(
    dp,
    tp,
    activations,
    cotangent,
    in_weight,
    in_first,
    in_second,
    step_weight,
    step_first,
    step_second,
    out_weight,
    out_first,
    out_second,
    state_weight,
    state_first,
    state_second,
    conv_weight,
    conv_first,
    conv_second,
    conv_bias,
    bias_first,
    bias_second,
    gain_vector,
    gains_first,
    gains_second,
    head_params,
    head_first,
    head_second,
):
    dp_rank = lax.axis_index("dp")
    rank = lax.axis_index("tensor")
    tokens, depth = activations.shape
    shard_rows, _, inner = in_weight.shape
    norm_width = inner * tp
    heads = step_weight.shape[1]
    head_width = inner // heads
    state_rows, conv_states = state_weight.shape
    conv = inner + conv_states
    taps, conv_own = conv_weight.shape
    gains_own = gain_vector.shape[0]
    sizes = (inner, head_width, heads)

    w_own = jnp.concatenate(
        [
            in_weight.reshape(shard_rows, 2 * inner).astype(BF16),
            pad_to(step_weight.astype(BF16), LANES),
            out_weight.astype(BF16).T,
        ],
        1,
    )
    padded_rows = -(-state_rows // 16) * 16
    st_own = jnp.pad(state_weight.astype(BF16), ((0, padded_rows - state_rows), (0, 0)))
    flat = jnp.concatenate([conv_weight.reshape(-1), conv_bias, gain_vector])
    sm_own = pad_to(flat, -(-flat.shape[0] // 1024) * 1024).reshape(-1, LANES)
    w, st_full, sm_full = run_gather(w_own, st_own, sm_own, dp, tp)
    ws = st_full[:, :, :state_rows].reshape(depth, conv_states)
    small = sm_full.reshape(dp * tp, -1)
    kernel_full = (
        small[:, : taps * conv_own].reshape(-1, taps, conv_own).transpose(1, 0, 2).reshape(taps, -1)
    )
    offsets_full = small[:, taps * conv_own : (taps + 1) * conv_own].reshape(-1)
    gains_full = small[:, (taps + 1) * conv_own : (taps + 1) * conv_own + gains_own].reshape(-1)
    start = rank * inner
    conv_rows = jnp.concatenate([kernel_full, offsets_full[None, :]], 0)
    conv_local = jnp.concatenate(
        [lax.dynamic_slice_in_dim(conv_rows, start, inner, 1), conv_rows[:, norm_width:]], 1
    )
    head_local = lax.dynamic_slice_in_dim(head_params, rank * heads, heads, 1)
    gain_local = lax.dynamic_slice_in_dim(gains_full, depth + start, inner, 0)
    pv = jnp.concatenate(
        [
            gains_full[None, :depth],
            pad_to(jnp.concatenate([gain_local, jnp.repeat(head_local[2], head_width)]), depth)[
                None, :
            ],
            pad_to(conv_local, depth),
            pad_to(
                jnp.concatenate(
                    [pad_to(-jnp.exp(head_local[0]), LANES), pad_to(head_local[1], LANES)]
                ),
                depth,
            )[None, :],
        ],
        0,
    )

    sums, _, _, _, _, _, _, _, _, own, vectors, head_sums, totals = run_mixer(
        activations, cotangent, w, ws, pv, dp, tp, sizes, norm_width
    )
    block_output, input_grad = run_finalize(activations, cotangent, sums, totals, norm_width)

    in_owned = own[:, : 2 * inner].reshape(shard_rows, 2, inner)
    state_part = own[:, 2 * inner : inner + conv]
    step_owned = own[:, inner + conv : inner + conv + heads].T
    out_owned = own[:, inner + conv + LANES :].T
    state_owned = lax.dynamic_slice_in_dim(state_part, rank * state_rows, state_rows, 0)
    for k in range(1, tp):
        theirs = lax.dynamic_slice_in_dim(state_part, (rank ^ k) * state_rows, state_rows, 0)
        state_owned = state_owned + swap(theirs, k, tp)

    head_grad = head_sums[:, :3, :heads].transpose(1, 0, 2).reshape(3, tp * heads)
    device = dp_rank * tp + rank
    conv_owned = lax.dynamic_slice(vectors, (0, device * conv_own), (taps + 1, conv_own))
    gains_owned = lax.dynamic_slice(vectors, (taps + 1, device * gains_own), (1, gains_own))[0]

    in_new = adamw_update(in_weight, in_owned, in_first, in_second, RATE_MATRIX, WEIGHT_DECAY)
    step_new = adamw_update(
        step_weight.T, step_owned, step_first.T, step_second.T, RATE_MATRIX, WEIGHT_DECAY
    )
    step_new = tuple(value.T for value in step_new)
    out_new = adamw_update(out_weight, out_owned, out_first, out_second, RATE_OUTPUT, WEIGHT_DECAY)
    state_new = adamw_update(
        state_weight, state_owned, state_first, state_second, RATE_MATRIX, WEIGHT_DECAY
    )
    conv_new = adamw_update(conv_weight, conv_owned[:taps], conv_first, conv_second, RATE_CONV, 0.0)
    bias_new = adamw_update(conv_bias, conv_owned[taps], bias_first, bias_second, RATE_VECTOR, 0.0)
    gains_new = adamw_update(gain_vector, gains_owned, gains_first, gains_second, RATE_VECTOR, 0.0)
    head_new = adamw_update(head_params, head_grad, head_first, head_second, RATE_HEADS, 0.0)
    return (
        (block_output, input_grad)
        + in_new
        + step_new
        + out_new
        + state_new
        + conv_new
        + bias_new
        + gains_new
        + head_new
    )


def solution(mesh):
    both = ("dp", "tensor")
    rows = P("dp", None)
    projection = P("dp", None, "tensor")
    step = P("dp", "tensor")
    out = P("tensor", "dp")
    state = P(both, None)
    taps = P(None, both)
    vector = P(both)
    parameters = sum(
        ((spec,) * 3 for spec in (projection, step, out, state, taps, vector, vector, P())), ()
    )
    return jax.shard_map(
        functools.partial(shards, mesh.shape["dp"], mesh.shape["tensor"]),
        mesh=mesh,
        in_specs=(rows, rows) + parameters,
        out_specs=(rows, rows) + parameters,
        check_vma=False,
    )
```

time: 1880 us -> 497 us (0.26)
  waiting for transfers between devices: 786 us -> 0.01 us
  Pallas kernels: 0 us -> 451 us
  matrix products: 356 us -> 0 us
  local copies, waits for them, and re-layouts: 257 us -> 17.6 us
  other arithmetic: 248 us -> 20.5 us
  blocking collectives: 199 us -> 0 us
    pallas_call x0 -> x3, Pallas kernels: none -> 451 us  [the longest x1 383 us: run_mixer(): pl.pallas_call(functools.partial(mixer, dp=dp, tp=tp, sizes=sizes, norm_w...]
    psum x2 -> x0, waiting for transfers between devices: 430 us -> none  [the longest x1 219 us: shards(): lax.psum(input_part.astype(jnp.bfloat16), 'tensor').astype(jnp.float32)]
    dot_general x68 -> x0, matrix products: 356 us -> none  [the longest x12 111 us: one_block(): within = jnp.einsum('hts,shp->thp', mixing, block_values, precision=HIGHEST)]
    unnamed x12 -> x0, waiting for transfers between devices: 186 us -> none
    all_gather x3 -> x0, blocking collectives: 148 us -> none  [the longest x1 72.1 us: shards(): lax.all_gather(state_weight, ('dp', 'tensor'), axis=0, tiled=True)]
    reduce_scatter x2 -> x0, waiting for transfers between devices: 140 us -> none  [the longest x1 100 us: shards(): lax.psum_scatter(state_wgrad, ('dp', 'tensor'), scatter_dimension=0, tile...]
    reduce_sum x11 -> x0, other arithmetic: 59.1 us -> none  [the longest x1 17.1 us: causal_conv(): kernel[shift_tap][None, :] * padded[shift_tap:shift_tap + length]]
    another operation x41 -> x0, other arithmetic: 47.3 us -> none
  transfers between devices with their start and end apart: 9 -> 3, of which waited for: 8 -> 0; matrix products, arithmetic and copies ran while one was open for 5% -> 4% of each run, Pallas kernels for 0% -> 3%
where the time goes in v1:
time: 497 us; the launch traced here: 494 us
  Pallas kernels  451 us (91%)
  other arithmetic  20.5 us (4%)
  local copies, waits for them, and re-layouts  17.6 us (4%)
    pallas_call x1, Pallas kernels, run_mixer(): pl.pallas_call(functools.partial(mixer, dp=dp, tp=tp, sizes=sizes, norm_w...  383 us
    pallas_call x1, Pallas kernels, run_gather(): pl.pallas_call(functools.partial(gather_weights, dp=dp, tp=tp, cut=cut),...  53.9 us
    sub x8, other arithmetic, adamw_update(): return (weight - step_rate * (update + decay_rate * weight), moment, square)  14.8 us
    pallas_call x1, Pallas kernels, run_finalize(): pl.pallas_call(functools.partial(finalize, norm_width=norm_width), grid=(...  13.5 us
  transfers between devices with their start and end apart: 3, of which 0 were waited for; matrix products, arithmetic and copies ran while one was open for 4% of the time, Pallas kernels for 3%

profile of v1, /device:TPU:0, one launch (start us, length us, event | category | flops | bytes accessed | tf_op | source)
XLA Modules:
  0.0 494.4 jit_solution(9160680781594370326)
XLA Ops:
  0.7 0.8 broadcast_multiply_fusion.1
  1.6 1.7 convert_element_type.26
  4.9 1.0 fusion.4.w_own
  6.5 53.9 %gather_weights.1 = (bf16[1536,2432]{1,0:T(8,128)(2,1)}, bf16[8,4,48,256]{3,2,1,0:T(8,128)(2,1)}, f32[8,4,8,128]{3,2,1,0:T(8,128)}) custom-call(bf16[192,2432]{1,0:T(8,128)(2,1)} %fusion.4.w_own, bf16[48,256]{1,0:T(8,128)(2,1)} %convert_element_type.30.st_own, f32[8,128]{1,0:T(8,128)} %fusion.13.sm_own), custom_call_target="tpu_custom_call" | custom-call | tf_op jit(solution)/shard_map/gather_weights/pallas_call | solution.py:223
  60.5 0.9 copy.92
  63.1 383.5 %mixer.1 = (bf16[16,2,128,1536]{3,2,1,0:T(8,128)(2,1)}, bf16[16,2,128,1536]{3,2,1,0:T(8,128)(2,1)}, bf16[16,2,128,1536]{3,2,1,0:T(8,128)(2,1)}, bf16[4,192,2688]...) custom-call(bf16[2048,1536]{1,0:T(8,128)(2,1)} %x_ref.1, ...), custom_call_target="tpu_custom_call" | custom-call | flops 95026151424 | bytes 60000000 | tf_op jit(solution)/shard_map/mixer/pallas_call | solution.py:1104
  446.6 0.9 slice.56
  448.2 2.8 collective-permute-start.1
  451.0 1.6 collective-permute-start.2
  452.7 1.4 slice.53
  454.1 0.8 constant_dynamic-slice_fusion
  454.9 1.3 constant_dynamic-slice_fusion.5
  456.6 0.8 reshape.94
  457.4 0.7 slice_bitcast_fusion
  458.2 1.3 add_subtract_fusion
  459.5 1.2 multiply_subtract_fusion.6
  460.7 3.0 multiply_subtract_fusion.1
  463.9 5.6 %multiply_subtract_fusion = (f32[192,2,768]{2,1,0:T(2,128)}, f32[192,2,768]{2,1,0:T(2,128)}, f32[192,2,768]{2,1,0:T(2,128)}) fusion(f32[192,2,768]{2,1,0:T(2,128)S(1)} %copy-done.3, f32[192,2,768]{2,1,0:T(2,128)S(1)} %reshape.94, f32[192,2,768]{2,1,0:T(2,128)S(1)} %copy-done.5, f32[192,2,768]{2,1,0:T(2,128)S(1)} %copy-done.6), kind=kLoop, calls=%fused_computation.6 | loop fusion | flops 4423680 | bytes 8257536 | tf_op jit(solution)/shard_map/sub | solution.py:1189
  470.0 1.0 multiply_subtract_fusion.2
  472.3 0.7 copy.86
  473.7 2.8 copy-done
  476.5 2.8 copy-done.1
  479.3 13.5 %finalize.1 = (bf16[2048,1536]{1,0:T(8,128)(2,1)}, f32[2048,1536]{1,0:T(8,128)}) custom-call(bf16[2048,1536]{1,0:T(8,128)(2,1)S(1)} %copy-done, bf16[2048,1536]{1,0:T(8,128)(2,1)S(1)} %copy-done.1, bf16[16,2,128,1536]{3,2,1,0:T(8,128)(2,1)} %get-tuple-element.39.out_ref.in_ref, bf16[16,2,128,1536]{3,2,1,0:T(8,128)(2,1)} %get-tuple-element.39.out_ref.in_ref, ...), custom_call_target="tpu_custom_call" | custom-call | flops 18874368 | bytes 44040192 | tf_op jit(solution)/shard_map/finalize/pallas_call | solution.py:1064
  492.8 1.5 multiply_subtract_fusion.3
  (92 shorter events, 7.8 us)
Async XLA Ops:
  1.6 1.8 copy-start.4
  4.2 1.7 copy-start.21
  5.9 55.9 %copy-start.15 = (f32[3,48]{1,0:T(4,128)S(1)}, f32[3,48]{1,0:T(4,128)}, u32[]{:S(2)}) copy-start(f32[3,48]{1,0:T(4,128)} %param.49) | copy-start | bytes 1732
  63.1 389.5 %copy-start.9 = (f32[192,12]{0,1:T(8,128)S(1)}, f32[192,12]{0,1:T(8,128)}, u32[]{:S(2)}) copy-start(f32[192,12]{0,1:T(8,128)} %param.31) | copy-start | bytes 27652
  448.2 44.6 %collective-permute-start = (f32[48,256]{1,0:T(8,128)}, f32[48,256]{1,0:T(8,128)}, u32[]{:S(2)}, u32[]{:S(2)}) collective-permute-start(f32[48,256]{1,0:T(8,128)} %get-tuple-element.148), channel_id=1, source_target_pairs={{0,1},{1,0},{2,3},{3,2},{4,5},{5,4},{6,7},{7,6},{8,9},{9,8},{10,11... | collective-permute-start | bytes 147464 | tf_op jit(solution)/shard_map/ppermute | solution.py:1193
  448.2 44.6 %collective-permute-start.1 = (f32[48,256]{1,0:T(8,128)}, f32[48,256]{1,0:T(8,128)}, u32[]{:S(2)}, u32[]{:S(2)}) collective-permute-start(f32[48,256]{1,0:T(8,128)} %get-tuple-element.150), channel_id=1, source_target_pairs={{0,2},{1,3},{2,0},{3,1},{4,6},{5,7},{6,4},{7,5},{8,10},{9,11},{10,... | collective-permute-start | bytes 147464 | tf_op jit(solution)/shard_map/ppermute | solution.py:1193
  451.0 41.8 %collective-permute-start.2 = (f32[48,256]{1,0:T(8,128)}, f32[48,256]{1,0:T(8,128)}, u32[]{:S(2)}, u32[]{:S(2)}) collective-permute-start(f32[48,256]{1,0:T(8,128)} %get-tuple-element.149), channel_id=1, source_target_pairs={{0,3},{1,2},{2,1},{3,0},{4,7},{5,6},{6,5},{7,4},{8,11},{9,10},{10,... | collective-permute-start | bytes 147464 | tf_op jit(solution)/shard_map/ppermute | solution.py:1193
  452.7 3.6 copy-start.12
  452.7 3.7 copy-start.13
  460.7 3.1 copy-start.3
  460.7 3.1 copy-start.5
  460.7 3.1 copy-start.6
  463.8 5.6 %copy-start.19 = (f32[3,48]{1,0:T(4,128)S(1)}, f32[3,48]{1,0:T(4,128)}, u32[]{:S(2)}) copy-start(f32[3,48]{1,0:T(4,128)} %param.50) | copy-start | bytes 1732
  463.8 5.6 %copy-start.20 = (f32[3,48]{1,0:T(4,128)S(1)}, f32[3,48]{1,0:T(4,128)}, u32[]{:S(2)}) copy-start(f32[3,48]{1,0:T(4,128)} %param.51) | copy-start | bytes 1732
  463.8 7.2 %copy-start.17 = (f32[144]{0:T(256)S(1)}, f32[144]{0:T(256)}, u32[]{:S(2)}) copy-start(f32[144]{0:T(256)} %param.46) | copy-start | bytes 1732
  463.8 7.2 %copy-start.18 = (f32[1,144]{1,0:T(1,128)S(1)}, f32[1,144]{1,0:T(1,128)}, u32[]{:S(2)}) copy-start(f32[1,144]{1,0:T(1,128)} %constant_dynamic-slice_fusion.5) | copy-start | bytes 1732
  463.8 7.2 %copy-start.22 = (f32[144]{0:T(256)S(1)}, f32[144]{0:T(256)}, u32[]{:S(2)}) copy-start(f32[144]{0:T(256)} %param.47) | copy-start | bytes 1732
  463.8 7.2 %copy-start.23 = (f32[144]{0:T(256)S(1)}, f32[144]{0:T(256)}, u32[]{:S(2)}) copy-start(f32[144]{0:T(256)} %param.48) | copy-start | bytes 1732
  469.4 4.3 copy-start.2
  473.7 2.8 copy-start
  476.5 2.8 copy-start.1
  479.3 13.6 %copy-start.8 = (f32[48,256]{1,0:T(8,128)S(1)}, f32[48,256]{1,0:T(8,128)}, u32[]{:S(2)}) copy-start(f32[48,256]{1,0:T(8,128)} %param.37) | copy-start | bytes 147460
  479.3 13.6 %copy-start.10 = (f32[48,256]{1,0:T(8,128)S(1)}, f32[48,256]{1,0:T(8,128)}, u32[]{:S(2)}) copy-start(f32[48,256]{1,0:T(8,128)} %param.38) | copy-start | bytes 147460
  479.3 13.6 %copy-start.11 = (f32[48,256]{1,0:T(8,128)S(1)}, f32[48,256]{1,0:T(8,128)}, u32[]{:S(2)}) copy-start(f32[48,256]{1,0:T(8,128)} %param.39) | copy-start | bytes 147460
  (3 other events, 3.9 us)

commit v2 on v1

--- a/solution.py
+++ b/solution.py
@@ -326,7 +326,7 @@
 
 
 def backward_step(
-    f, x, c, w_v, ws_v, pv, totals, saved, dst_v, dext, small, grads, lowered_v, turned, put, stage, sizes, norm_width
+    f, x, c, w_v, ws_v, pv, totals, saved, dst_v, dext, small, grads, lowered_v, turned, put, between, stage, sizes, norm_width
 ):
     inner, head_width, heads = sizes
     cin_s, pre_s, gate_s, y_s, sp_s, state_s = saved
@@ -414,6 +414,8 @@
             mixing = (fade * inter).astype(BF16)
             inter_grad = inter_grad + mm_nt((yp * mask).astype(BF16), xp) * fade
             parts.append(mm(yb_t[h * head_width : (h + 1) * head_width, :], mixing))
+        if pair == heads // 4:
+            between()
     xd_grad = jnp.transpose(jnp.concatenate(parts, 0)) + b_state
     inter_low = (inter_grad * causal).astype(BF16)
     c_grad = c_grad + mm(inter_low, bmat)
@@ -481,6 +483,7 @@
     branch_hbm,
     normed_hbm,
     own,
+    state_sum,
     vectors,
     head_sums,
     totals,
@@ -504,7 +507,8 @@
     lowered_v,
     turned,
     stage,
-    landed,
+    edge_v,
+    across_v,
     mine_v,
     pair,
     total_v,
@@ -514,6 +518,7 @@
     small1,
     small2,
     small3,
+    state_in,
     w_sem,
     load_sem,
     edge_send,
@@ -534,6 +539,8 @@
     tile_sem,
     sm_send,
     sm_recv,
+    st_send,
+    st_recv,
     *,
     dp,
     tp,
@@ -634,101 +641,109 @@
             device_id_type=MESH,
         )
 
-    def landing(source, n, h):
-        return pltpu.make_async_copy(source.at[slot_of(n), h], landed.at[h], pump_sem.at[h])
-
-    def mine_load(n):
-        return pltpu.make_async_copy(mine.at[slot_of(n)], mine_v, pump_sem.at[2])
+    def edge_load(n, h):
+        return pltpu.make_async_copy(edge.at[slot_of(n), h], edge_v.at[h], pump_sem.at[0, h])
+
+    def across_load(n, h):
+        return pltpu.make_async_copy(across.at[slot_of(n), h], across_v.at[h], pump_sem.at[1, h])
+
+    def mine_load(n, h):
+        return pltpu.make_async_copy(mine.at[slot_of(n), h], mine_v.at[h], pump_sem.at[2, h])
 
     def store_piece(n):
         return pltpu.make_async_copy(stage, mine.at[slot_of(n)], mine_sem.at[0])
 
-    def in_groups(apart, arrived, load, place, send):
-        for group in ((0,), (1,)) if apart else ((0, 1),):
-            for h in group:
-                arrived(h)
-            for h in group:
-                load(h).start()
-            for h in group:
-                load(h).wait()
-            for h in group:
-                place(h)
-                send(h)
-
-    def combine(n, apart=False):
-        mine_load(n).start()
-
+    def begin_combine(n, h):
+        inward(n, h).wait_recv()
+        edge_load(n, h).start()
+        mine_load(n, h).start()
+
+    def end_combine(n, h):
         @pl.when(n >= 2)
         def _():
-            for h in (0, 1):
-                across_copy(n - 2, h).wait_send()
-
-        mine_load(n).wait()
-        slot = lax.rem(n, 2)
-
-        def place(h):
-            pair[slot, h] = add_low(mine_v[h], landed[h])
-
-        in_groups(
-            apart,
-            lambda h: inward(n, h).wait_recv(),
-            lambda h: landing(edge, n, h),
-            place,
-            lambda h: across_copy(n, h).start(),
-        )
-
-    def finish(n, apart=False):
+            across_copy(n - 2, h).wait_send()
+
+        edge_load(n, h).wait()
+        mine_load(n, h).wait()
+        pair[lax.rem(n, 2), h] = add_low(mine_v[h], edge_v[h])
+        across_copy(n, h).start()
+
+    def begin_finish(n, h):
+        across_copy(n, h).wait_recv()
+        across_load(n, h).start()
+
+    def end_finish(n, h):
         @pl.when(n >= 2)
         def _():
-            for h in (0, 1):
-                outward(n - 2, h).wait_send()
-                kept(n - 2, h).wait()
-
+            outward(n - 2, h).wait_send()
+            kept(n - 2, h).wait()
+
+        across_load(n, h).wait()
         slot = lax.rem(n, 2)
-
-        def place(h):
-            total_v[slot, h] = add_low(pair[slot, h], landed[h])
-
-        def send(h):
-            outward(n, h).start()
-            kept(n, h).start()
-
-        in_groups(
-            apart,
-            lambda h: across_copy(n, h).wait_recv(),
-            lambda h: landing(across, n, h),
-            place,
-            send,
-        )
-
-    def combined(n):
-        return jnp.maximum(2 * n - 3, 0) // 3
-
-    def sent(n):
-        paced = combined(n) + 2 + lax.rem(n, cycle) // per
-        return jnp.where(n == pieces - 1, pieces, jnp.where(n < 0, 0, jnp.minimum(n + 1, paced)))
-
-    def pump(n):
+        total_v[slot, h] = add_low(pair[slot, h], across_v[h])
+        outward(n, h).start()
+        kept(n, h).start()
+
+    ticks = 3 * per + 1
+
+    def made(tick):
+        s, q = (tick - 1) // ticks, lax.rem(tick - 1, ticks) + 1
+        return cycle * s + jnp.minimum(q, per) + jnp.maximum(q - per - 1, 0) // 2
+
+    def combined(tick):
+        return jnp.maximum(3 * tick - 4, 0) // 7
+
+    def finished(tick):
+        return combined(jnp.maximum(tick - 4, 0))
+
+    def sent(tick):
+        paced = jnp.minimum(made(jnp.maximum(tick, 1)), (3 * tick + 9) // 7)
+        return jnp.where(tick == ticks * sequences, pieces, jnp.where(tick < 1, 0, paced))
+
+    def pump(tick):
         @pl.when(is_end)
         def _():
-            @pl.loop(sent(n - 1), sent(n))
+            @pl.loop(sent(tick - 1), sent(tick))
             def _(k):
                 for h in (0, 1):
                     inward(k, h).start()
 
-        @pl.when(is_middle & (combined(n - 2) > combined(n - 3)))
+        def middle(count, when, step):
+            @pl.when(is_middle & (when >= 1) & (count(when) > count(when - 1)))
+            def _():
+                for h in (0, 1):
+                    step(count(when) - 1, h)
+
+        middle(finished, tick - 1, end_finish)
+        middle(combined, tick - 1, end_combine)
+        middle(finished, tick, begin_finish)
+        middle(combined, tick, begin_combine)
+
+    def combine(n, apart=False):
+        for group in ((0,), (1,)) if apart else ((0, 1),):
+            for h in group:
+                begin_combine(n, h)
+            for h in group:
+                end_combine(n, h)
+
+    def finish(n, apart=False):
+        for group in ((0,), (1,)) if apart else ((0, 1),):
+            for h in group:
+                begin_finish(n, h)
+            for h in group:
+                end_finish(n, h)
+
+    def free_stage(n):
+        @pl.when(is_middle & (n >= 1))
         def _():
-            finish(combined(n - 2) - 1)
-
-        @pl.when(is_middle & (combined(n) > combined(n - 1)))
+            store_piece(n - 1).wait()
+
+    def keep_piece(n):
+        store_piece(n).start()
+
+        @pl.when(is_end)
         def _():
-            combine(combined(n) - 1)
-
-    def advance(n, apart=False):
-        @pl.when(is_middle)
-        def _():
-            combine(n, apart)
-            finish(n - 1, apart)
+            store_piece(n).wait()
 
     def puts(b, which):
         pairs = (
@@ -768,6 +783,7 @@
         def _(f):
             n = first_n + f
             next_block(n)
+            free_stage(n)
             slot = lax.rem(n, 2)
             forward_step(
                 f,
@@ -784,18 +800,18 @@
                 sizes,
             )
 
-            store_piece(n).start()
+            keep_piece(n)
 
             @pl.when(f == per - 1)
             def _():
                 for k in range(1, tp):
                     stat_copy(s, k).start()
 
-            store_piece(n).wait()
-            pump(n)
+            pump(ticks * s + 1 + f)
 
         for k in range(1, tp):
             stat_copy(s, k).wait()
+        pump(ticks * s + per + 1)
         ext[SPAN:, :] = jnp.zeros((8, conv), F32)
         dst_v[...] = jnp.zeros_like(dst_v)
         totals[s] = (stat_own[s] + stat_in[s, 0]) + (stat_in[s, 1] + stat_in[s, 2])
@@ -805,7 +821,9 @@
             n = first_n + per + j
             f = per - 1 - j
             b = per * s + f
+            tick = ticks * s + per + 1 + 2 * j
             next_block(n)
+            free_stage(n)
 
             @pl.when(b != per - 1)
             def _():
@@ -829,13 +847,13 @@
                 lowered_v,
                 turned,
                 puts(b, range(4)),
+                lambda: pump(tick + 1),
                 stage,
                 sizes,
                 norm_width,
             )
-            store_piece(n).start()
-            store_piece(n).wait()
-            pump(n)
+            keep_piece(n)
+            pump(tick + 2)
 
     def to_sibling(q):
         at = pl.multiple_of((2 * q + 1 - parity) * rows, 16)
@@ -907,6 +925,19 @@
 
     for copy in puts(per * (sequences - 1), (0, 1, 3)):
         copy.wait()
+    last_tick = ticks * sequences
+    count = lambda tick: max(3 * tick - 4, 0) // 7
+    done_finish, done_combine = count(last_tick - 4), count(last_tick)
+
+    @pl.when(is_middle)
+    def _():
+        store_piece(pieces - 1).wait()
+        for h in (0, 1):
+            if count(last_tick - 4) > count(last_tick - 5):
+                end_finish(done_finish - 1, h)
+            if count(last_tick) > count(last_tick - 1):
+                end_combine(done_combine - 1, h)
+
     for copy in left_operand(normed_hbm):
         copy.start()
     tile_load(grads_hbm, 0, 256, 0).start()
@@ -924,14 +955,25 @@
         copy.start()
     tile_load(lowered_hbm, 0, 256, 0).start()
 
-    head = (2 * (pieces - 1) - 3) // 3
-
-    @pl.when(is_middle)
-    def _():
-        for n in range((2 * (pieces - 3) - 3) // 3, head - 1):
-            finish(n)
-
-    advance(head)
+    steps, behind = [], done_finish
+    for n in range(done_combine, pieces):
+        while behind <= n - 2:
+            steps.append((finish, behind))
+            behind += 1
+        steps.append((combine, n))
+    steps += [(finish, n) for n in range(behind, pieces)]
+
+    def drain(upto):
+        count = steps.index((combine, upto)) + 1 if upto < pieces else len(steps)
+
+        @pl.when(is_middle)
+        def _():
+            for step, n in steps[:count]:
+                step(n, n >= pieces - 2)
+
+        del steps[:count]
+
+    drain(done_combine)
     for copy in left_operand(branch_hbm):
         copy.wait()
     products(lowered_hbm, inner, wide)
@@ -942,10 +984,7 @@
 
     first_small = small_copy(small, small1, 0, (sibling, z))
     first_small.start()
-    spread_over = pieces - 1 - head
-    early = head + 1 + max(spread_over // 3, 0)
-    for n in range(head + 1, early):
-        advance(n)
+    drain(done_combine + 2)
     first_small.wait()
     small2[chip] = small[...] + small1[...]
     second_small = [
@@ -967,9 +1006,7 @@
         ).astype(BF16)
         to_owner(k).start()
 
-    late = max(early, pieces - 2)
-    for n in range(early, late):
-        advance(n)
+    drain(pieces - 2)
     to_sibling(chip).wait_recv()
     own[...] = wgrad[pl.ds(pl.multiple_of(me * rows, 16), rows), :].astype(F32) + fetch(
         rs1.at[chip]
@@ -986,15 +1023,36 @@
     ]
     for copy in third_small:
         copy.start()
-    for n in range(late, pieces - 1):
-        advance(n, True)
+    drain(pieces - 1)
 
     @pl.loop(1, half)
     def _(k):
         to_owner(k).wait_recv()
         own[...] += fetch(rs2.at[lax.rem(chip + half - k, half)])
 
-    advance(pieces - 1, True)
+    share = state_sum.shape[0]
+    state_columns = pl.ds(2 * inner, conv - inner)
+
+    def state_rows(device):
+        return pl.ds(pl.multiple_of(device * share, 8), share)
+
+    state_copies = [
+        pltpu.make_async_remote_copy(
+            src_ref=own.at[state_rows(flipped(z, k)), state_columns],
+            dst_ref=state_in.at[k - 1],
+            send_sem=st_send.at[k - 1],
+            recv_sem=st_recv.at[k - 1],
+            device_id=(me, flipped(z, k)),
+            device_id_type=MESH,
+        )
+        for k in range(1, tp)
+    ]
+    if share * tp == rows:
+        for copy in state_copies:
+            copy.start()
+    else:
+        state_copies = []
+
     for copy in third_small:
         copy.wait()
     vectors[...] = jnp.zeros_like(vectors)
@@ -1018,9 +1076,15 @@
     vectors[0:5, tp * inner : tp * inner + both] = shared
     vectors[5:6, 0:depth] = before
 
-    @pl.when(is_middle)
-    def _():
-        finish(pieces - 1, True)
+    for copy in state_copies:
+        copy.wait()
+    if state_copies:
+        state_sum[...] = own[state_rows(z), state_columns] + (
+            state_in[0] + (state_in[1] + state_in[2])
+        )
+    else:
+        state_sum[...] = jnp.zeros_like(state_sum)
+    drain(pieces)
 
     @pl.loop(0, half)
     def _(q):
@@ -1073,7 +1137,7 @@
         ],
         out_specs=(rows, rows),
         out_shape=(sds((tokens, depth), BF16), sds((tokens, depth), F32)),
-        compiler_params=pltpu.CompilerParams(vmem_limit_bytes=32 * 1024 * 1024),
+        compiler_params=pltpu.CompilerParams(vmem_limit_bytes=60 * 1024 * 1024),
         cost_estimate=pl.CostEstimate(
             flops=6 * tokens * depth, bytes_accessed=14 * tokens * depth, transcendentals=0
         ),
@@ -1100,11 +1164,12 @@
     dma = pltpu.SemaphoreType.DMA
     piece = (2, HALF, depth)
     rows_of_x = (SPAN, depth)
+    share = rows // tp if rows % (8 * tp) == 0 else 8
     flops = tokens * (6 * depth * (2 * inner + conv) + 6 * depth * inner + 80 * heads * SPAN * 64)
     return pl.pallas_call(
         functools.partial(mixer, dp=dp, tp=tp, sizes=sizes, norm_width=norm_width),
         in_specs=[hbm] * 4 + [vmem],
-        out_specs=(hbm,) * 9 + (vmem,) * 4,
+        out_specs=(hbm,) * 9 + (vmem,) * 5,
         out_shape=(
             sds((pieces,) + piece, BF16),
             sds((pieces,) + piece, BF16),
@@ -1116,6 +1181,7 @@
             sds((blocks, depth, SPAN), BF16),
             sds((blocks, depth, SPAN), BF16),
             sds((rows, wide + inner), F32),
+            sds((share, conv_states), F32),
             sds((8, tp * inner + depth), F32),
             sds((tp, 8, LANES), F32),
             sds((sequences, per, 8, SPAN), F32),
@@ -1143,6 +1209,7 @@
             pltpu.VMEM(piece, BF16),
             pltpu.VMEM(piece, BF16),
             pltpu.VMEM(piece, BF16),
+            pltpu.VMEM(piece, BF16),
             pltpu.VMEM((2,) + piece, BF16),
             pltpu.VMEM((2,) + piece, BF16),
             pltpu.VMEM((rows, wide + inner), BF16),
@@ -1151,6 +1218,7 @@
             pltpu.VMEM((8, depth), F32),
             pltpu.VMEM((half, 8, depth), F32),
             pltpu.VMEM((tp, 8, depth), F32),
+            pltpu.VMEM((tp - 1, share, conv_states), F32),
             dma((2,)),
             dma((2, 2)),
             dma((pieces, 2)),
@@ -1159,7 +1227,7 @@
             dma((pieces, 2)),
             dma((pieces, 2)),
             dma((1,)),
-            dma((3,)),
+            dma((3, 2)),
             dma((sequences, tp - 1)),
             dma((sequences, tp - 1)),
             dma((half,)),
@@ -1171,6 +1239,8 @@
             dma((2 + blocks,)),
             dma((half + tp,)),
             dma((half + tp,)),
+            dma((tp - 1,)),
+            dma((tp - 1,)),
         ],
         compiler_params=pltpu.CompilerParams(
             collective_id=2, has_side_effects=True, vmem_limit_bytes=MIXER_VMEM
@@ -1284,7 +1354,7 @@
         0,
     )
 
-    sums, _, _, _, _, _, _, _, _, own, vectors, head_sums, totals = run_mixer(
+    sums, _, _, _, _, _, _, _, _, own, state_sum, vectors, head_sums, totals = run_mixer(
         activations, cotangent, w, ws, pv, dp, tp, sizes, norm_width
     )
     block_output, input_grad = run_finalize(activations, cotangent, sums, totals, norm_width)
@@ -1293,11 +1363,13 @@
     state_part = own[:, 2 * inner : inner + conv]
     step_owned = own[:, inner + conv : inner + conv + heads].T
     out_owned = own[:, inner + conv + LANES :].T
-    state_owned = lax.dynamic_slice_in_dim(state_part, rank * state_rows, state_rows, 0)
-    for k in range(1, tp):
-        theirs = lax.dynamic_slice_in_dim(state_part, (rank ^ k) * state_rows, state_rows, 0)
-        state_owned = state_owned + swap(theirs, k, tp)
-
+    if state_sum.shape[0] == state_rows:
+        state_owned = state_sum
+    else:
+        state_owned = lax.dynamic_slice_in_dim(state_part, rank * state_rows, state_rows, 0)
+        for k in range(1, tp):
+            theirs = lax.dynamic_slice_in_dim(state_part, (rank ^ k) * state_rows, state_rows, 0)
+            state_owned = state_owned + swap(theirs, k, tp)
     head_grad = head_sums[:, :3, :heads].transpose(1, 0, 2).reshape(3, tp * heads)
     device = dp_rank * tp + rank
     conv_owned = lax.dynamic_slice(vectors, (0, device * conv_own), (taps + 1, conv_own))

time: 497 us -> 471 us (0.948)
  local copies, waits for them, and re-layouts: 17.6 us -> 7.76 us
  Pallas kernels: 451 us -> 443 us
    pallas_call x1, Pallas kernels: 383 us -> 372 us  [run_mixer(): pl.pallas_call(functools.partial(mixer, dp=dp, tp=tp, sizes=sizes, norm_w...]
    unnamed x54 -> x60, local copies, waits for them, and re-layouts: 9.49 us -> 3.79 us
  transfers between devices with their start and end apart: 3 -> 0, of which waited for: 0 -> 0; matrix products, arithmetic and copies ran while one was open for 4% -> 0% of each run, Pallas kernels for 3% -> 0%
where the time goes in v2:
time: 471 us; the launch traced here: 470 us
  Pallas kernels  443 us (94%)
  other arithmetic  18 us (4%)
  local copies, waits for them, and re-layouts  7.76 us (2%)
    pallas_call x1, Pallas kernels, run_mixer(): pl.pallas_call(functools.partial(mixer, dp=dp, tp=tp, sizes=sizes, norm_w...  372 us
    pallas_call x1, Pallas kernels, run_gather(): pl.pallas_call(functools.partial(gather_weights, dp=dp, tp=tp, cut=cut),...  53.9 us
    pallas_call x1, Pallas kernels, run_finalize(): pl.pallas_call(functools.partial(finalize, norm_width=norm_width), grid=(...  16.9 us
    sub x8, other arithmetic, adamw_update(): return (weight - step_rate * (update + decay_rate * weight), moment, square)  12.4 us

profile of v2, /device:TPU:0, one launch (start us, length us, event | category | flops | bytes accessed | tf_op | source)
XLA Modules:
  0.0 469.6 jit_solution(7499378068695841774)
XLA Ops:
  0.7 0.8 broadcast_multiply_fusion.1
  1.6 1.7 convert_element_type.26
  3.5 1.0 fusion.4.w_own
  4.5 0.6 convert_element_type.30.st_own
  5.2 0.7 fusion.13.sm_own
  5.9 53.9 %gather_weights.1 = (bf16[1536,2432]{1,0:T(8,128)(2,1)}, bf16[8,4,48,256]{3,2,1,0:T(8,128)(2,1)}, f32[8,4,8,128]{3,2,1,0:T(8,128)}) custom-call(bf16[192,2432]{1,0:T(8,128)(2,1)} %fusion.4.w_own, bf16[48,256]{1,0:T(8,128)(2,1)} %convert_element_type.30.st_own, f32[8,128]{1,0:T(8,128)} %fusion.13.sm_own), custom_call_target="tpu_custom_call" | custom-call | tf_op jit(solution)/shard_map/gather_weights/pallas_call | solution.py:223
  59.8 0.9 copy.92
  61.9 0.6 fusion.9.pv
  62.5 371.8 %mixer.1 = (bf16[16,2,128,1536]{3,2,1,0:T(8,128)(2,1)}, bf16[16,2,128,1536]{3,2,1,0:T(8,128)(2,1)}, bf16[16,2,128,1536]{3,2,1,0:T(8,128)(2,1)}, bf16[4,192,2688]...) custom-call(bf16[2048,1536]{1,0:T(8,128)(2,1)} %x_ref.1, ...), custom_call_target="tpu_custom_call" | custom-call | flops 95026151424 | bytes 60000000 | tf_op jit(solution)/shard_map/mixer/pallas_call | solution.py:1169
  434.4 16.9 %finalize.1 = (bf16[2048,1536]{1,0:T(8,128)(2,1)}, f32[2048,1536]{1,0:T(8,128)}) custom-call(bf16[2048,1536]{1,0:T(8,128)(2,1)} %x_ref.1, bf16[2048,1536]{1,0:T(8,128)(2,1)} %c_ref.1, bf16[16,2,128,1536]{3,2,1,0:T(8,128)(2,1)} %get-tuple-element.40.out_ref.in_ref, bf16[16,2,128,1536]{3,2,1,0:T(8,128)(2,1)} %get-tuple-element.40.out_ref.in_ref, ...), custom_call_target="tpu_custom_call" | custom-call | flops 18874368 | bytes 44040192 | tf_op jit(solution)/shard_map/finalize/pallas_call | solution.py:1128
  451.4 0.8 constant_dynamic-slice_fusion
  452.2 0.6 add_subtract_fusion
  452.8 0.5 multiply_subtract_fusion.6
  453.3 0.8 constant_dynamic-slice_fusion.2
  454.1 0.6 multiply_subtract_fusion.5
  455.3 0.7 copy.85
  455.9 0.7 copy.86
  456.6 0.7 copy.87
  457.5 0.8 reshape.94
  458.3 0.5 copy-done
  458.7 6.6 %multiply_subtract_fusion = (f32[192,2,768]{2,1,0:T(2,128)}, f32[192,2,768]{2,1,0:T(2,128)}, f32[192,2,768]{2,1,0:T(2,128)}) fusion(f32[192,2,768]{2,1,0:T(2,128)S(1)} %copy-done, f32[192,2,768]{2,1,0:T(2,128)S(1)} %reshape.94, f32[192,2,768]{2,1,0:T(2,128)} %param.29, f32[192,2,768]{2,1,0:T(2,128)} %param.30), kind=kLoop, calls=%fused_computation.6 | loop fusion | flops 4423680 | bytes 8257536 | tf_op jit(solution)/shard_map/sub | solution.py:1259
  465.5 2.7 multiply_subtract_fusion.1
  468.2 0.7 multiply_subtract_fusion.3
  468.9 0.6 multiply_subtract_fusion.4
  (90 shorter events, 2.2 us)
Async XLA Ops:
  1.6 1.8 copy-start.1
  3.5 1.7 copy-start.16
  3.5 1.7 copy-start.22
  4.5 56.5 %copy-start.15 = (f32[3,48]{1,0:T(4,128)S(1)}, f32[3,48]{1,0:T(4,128)}, u32[]{:S(2)}) copy-start(f32[3,48]{1,0:T(4,128)} %param.49) | copy-start | bytes 1732
  434.3 17.8 %copy-start.18 = (f32[4,104]{1,0:T(4,128)S(1)}, f32[4,104]{1,0:T(4,128)}, u32[]{:S(2)}) copy-start(f32[4,104]{1,0:T(4,128)} %param.41) | copy-start | bytes 4996
  434.3 17.8 %copy-start.19 = (f32[4,104]{1,0:T(4,128)S(1)}, f32[4,104]{1,0:T(4,128)}, u32[]{:S(2)}) copy-start(f32[4,104]{1,0:T(4,128)} %param.42) | copy-start | bytes 4996
  434.4 18.4 %copy-start.25 = (f32[104]{0:T(128)S(1)}, f32[104]{0:T(128)}, u32[]{:S(2)}) copy-start(f32[104]{0:T(128)} %param.44) | copy-start | bytes 1252
  434.4 18.4 %copy-start.26 = (f32[104]{0:T(128)S(1)}, f32[104]{0:T(128)}, u32[]{:S(2)}) copy-start(f32[104]{0:T(128)} %param.45) | copy-start | bytes 1252
  434.4 19.7 %copy-start.23 = (f32[144]{0:T(256)S(1)}, f32[144]{0:T(256)}, u32[]{:S(2)}) copy-start(f32[144]{0:T(256)} %param.47) | copy-start | bytes 1732
  434.4 19.7 %copy-start.24 = (f32[144]{0:T(256)S(1)}, f32[144]{0:T(256)}, u32[]{:S(2)}) copy-start(f32[144]{0:T(256)} %param.48) | copy-start | bytes 1732
  434.4 20.4 %copy-start.12 = (f32[192,12]{0,1:T(8,128)S(1)}, f32[192,12]{0,1:T(8,128)}, u32[]{:S(2)}) copy-start(f32[192,12]{0,1:T(8,128)} %param.32) | copy-start | bytes 27652
  434.4 20.5 %copy-start.13 = (f32[192,12]{0,1:T(8,128)S(1)}, f32[192,12]{0,1:T(8,128)}, u32[]{:S(2)}) copy-start(f32[192,12]{0,1:T(8,128)} %param.33) | copy-start | bytes 27652
  434.4 20.6 %copy-start.8 = (f32[192,12]{0,1:T(8,128)S(1)}, f32[192,12]{0,1:T(8,128)}, u32[]{:S(2)}) copy-start(f32[192,12]{0,1:T(8,128)} %param.31) | copy-start | bytes 27652
  434.4 20.7 %copy-start.3 = (f32[192,2688]{1,0:T(8,128)S(1)}, f32[192,2688]{1,0:T(8,128)}, u32[]{:S(2)}) copy-start(f32[192,2688]{1,0:T(8,128)} %get-tuple-element.44) | copy-start | bytes 6193156
  458.7 6.6 %copy-start.2 = (f32[768,192]{0,1:T(8,128)S(1)}, f32[768,192]{0,1:T(8,128)}, u32[]{:S(2)}) copy-start(f32[768,192]{0,1:T(8,128)} %param.34) | copy-start | bytes 1769476
  458.7 6.6 %copy-start.4 = (f32[768,192]{0,1:T(8,128)S(1)}, f32[768,192]{0,1:T(8,128)}, u32[]{:S(2)}) copy-start(f32[768,192]{0,1:T(8,128)} %param.35) | copy-start | bytes 1769476
  458.7 6.6 %copy-start.5 = (f32[768,192]{0,1:T(8,128)S(1)}, f32[768,192]{0,1:T(8,128)}, u32[]{:S(2)}) copy-start(f32[768,192]{0,1:T(8,128)} %param.36) | copy-start | bytes 1769476
  465.4 2.8 copy-start.7
  465.4 2.8 copy-start.9
  465.4 2.8 copy-start.10
  465.4 2.7 copy-start.11
  465.4 3.4 copy-start.17
  465.4 3.5 copy-start.20
  465.4 3.5 copy-start.21
  (3 other events, 4.0 us)

commit v3 on v2

--- a/solution.py
+++ b/solution.py
@@ -37,14 +37,16 @@
     return lax.dot_general(a, b, (((1,), (1,)), ((), ())), preferred_element_type=F32)
 
 
-def mm_exact(a, b):
-    return lax.dot_general(
-        a, b, (((1,), (0,)), ((), ())), preferred_element_type=F32, precision=lax.Precision.HIGHEST
-    )
+def mm_ones(ones, v):
+    high, low = split_low(v)
+    rest = (v - high.astype(F32) - low.astype(F32)).astype(BF16)
+    parts = mm(ones, jnp.concatenate([high, low, rest], 1))
+    width = v.shape[1]
+    return parts[:, 0:width] + parts[:, width : 2 * width] + parts[:, 2 * width :]
 
 
 def sigmoid(v):
-    return 1.0 / (1.0 + jnp.exp(-v))
+    return 0.5 * jnp.tanh(0.5 * v) + 0.5
 
 
 def softplus(v):
@@ -84,7 +86,7 @@
     row = lax.broadcasted_iota(jnp.int32, (SPAN, SPAN), 0)
     col = lax.broadcasted_iota(jnp.int32, (SPAN, SPAN), 1)
     keep = row >= col if lower else row <= col
-    return keep.astype(F32)
+    return keep.astype(F32).astype(BF16)
 
 
 def lane_masks():
@@ -115,7 +117,8 @@
 
 
 def gather_weights(
-    w_own, st_own, sm_own, w_full, st_full, sm_full, local_sem, z_send, z_recv, send_sem, recv_sem,
+    w_own, st_own, sm_own, w_full, st_full, sm_full,
+    local_sem, dp_send, dp_recv, z_send, z_recv, send_sem, recv_sem,
     *, dp, tp, cut
 ):
     me = lax.axis_index("dp")
@@ -124,51 +127,50 @@
     count = dp.bit_length() - 1
 
     barrier = pltpu.get_barrier_semaphore()
-    for b in range(count):
+    for k in range(1, dp):
         pl.semaphore_signal(
-            barrier, inc=1, device_id=(flipped(me, 1 << b), tensor), device_id_type=MESH
+            barrier, inc=1, device_id=(flipped(me, k), tensor), device_id_type=MESH
         )
     for k in range(1, tp):
         pl.semaphore_signal(barrier, inc=1, device_id=(me, flipped(tensor, k)), device_id_type=MESH)
-    pl.semaphore_wait(barrier, count + tp - 1)
-
-    order, other = axis_bits(dp)
-    row_of = lambda mask: pl.multiple_of(flipped(me, mask) * rows, 16)
-    left, right = pl.ds(0, cut), pl.ds(cut, width - cut)
-
-    def weight_part(columns):
-        def source(mask):
-            if mask == 0:
-                return w_own.at[:, columns]
-            return w_full.at[pl.ds(row_of(mask), rows), columns]
-
-        return source, lambda mask: w_full.at[pl.ds(row_of(mask), rows), columns]
-
-    state_part = (lambda mask: st_full.at[flipped(me, mask)],) * 2
-    small_part = (lambda mask: sm_full.at[flipped(me, mask)],) * 2
-    kinds = (
-        (order, weight_part(left)),
-        (other, weight_part(right)),
-        (order, state_part),
-        (other, small_part),
-    )
+    pl.semaphore_wait(barrier, dp + tp - 2)
+
+    orders = axis_bits(dp)
+    parts = (pl.ds(0, cut), pl.ds(cut, width - cut))
+
+    def row_of(mask):
+        return pl.multiple_of(flipped(me, mask) * rows, 16)
 
     def full_mask(bits, packed):
         return sum(1 << bits[j] for j in range(count) if packed >> j & 1)
 
     def move(kind, packed, j):
-        bits, (source, target) = kinds[kind]
+        bits, columns = orders[kind], parts[kind]
         mask = full_mask(bits, packed)
         slot = packed | (1 << j)
+        place = w_full.at[pl.ds(row_of(mask), rows), columns]
         return pltpu.make_async_remote_copy(
-            src_ref=source(mask),
-            dst_ref=target(mask),
+            src_ref=w_own.at[:, columns] if mask == 0 else place,
+            dst_ref=place,
             send_sem=send_sem.at[kind, slot],
             recv_sem=recv_sem.at[kind, slot],
             device_id=(flipped(me, 1 << bits[j]), tensor),
             device_id_type=MESH,
         )
 
+    smalls = ((st_own, st_full), (sm_own, sm_full))
+    direct = [
+        pltpu.make_async_remote_copy(
+            src_ref=own,
+            dst_ref=full.at[tensor, me],
+            send_sem=dp_send.at[which, k],
+            recv_sem=dp_recv.at[which, k],
+            device_id=(flipped(me, k), tensor),
+            device_id_type=MESH,
+        )
+        for k in range(1, dp)
+        for which, (own, full) in enumerate(smalls)
+    ]
     started = []
 
     def start(kind, packed, j):
@@ -176,42 +178,42 @@
         copy.start()
         started.append(copy)
 
-    zs = []
-    for k in range(1, tp):
-        for which, (own, full) in enumerate(((st_own, st_full), (sm_own, sm_full))):
-            copy = pltpu.make_async_remote_copy(
-                src_ref=own,
-                dst_ref=full.at[me, tensor],
-                send_sem=z_send.at[which, k],
-                recv_sem=z_recv.at[which, k],
-                device_id=(me, flipped(tensor, k)),
-                device_id_type=MESH,
-            )
-            copy.start()
-            zs.append(copy)
+    kept = [
+        pltpu.make_async_copy(own, full.at[tensor, me], local_sem.at[which])
+        for which, (own, full) in enumerate(smalls)
+    ]
+    kept.append(pltpu.make_async_copy(w_own, w_full.at[pl.ds(row_of(0), rows)], local_sem.at[2]))
+    for copy in direct:
+        copy.start()
     for j in range(count):
         for kind in (0, 1):
             start(kind, 0, j)
-    locals_ = [
-        pltpu.make_async_copy(w_own, w_full.at[pl.ds(row_of(0), rows)], local_sem.at[0]),
-        pltpu.make_async_copy(st_own, st_full.at[me, tensor], local_sem.at[1]),
-        pltpu.make_async_copy(sm_own, sm_full.at[me, tensor], local_sem.at[2]),
+    for copy in kept:
+        copy.start()
+    for copy in kept + direct:
+        copy.wait()
+    along = [
+        pltpu.make_async_remote_copy(
+            src_ref=full.at[tensor],
+            dst_ref=full.at[tensor],
+            send_sem=z_send.at[which, k],
+            recv_sem=z_recv.at[which, k],
+            device_id=(me, flipped(tensor, k)),
+            device_id_type=MESH,
+        )
+        for k in range(1, tp)
+        for which, (own, full) in enumerate(smalls)
     ]
-    for copy in locals_:
+    for copy in along:
         copy.start()
-    for copy in locals_:
-        copy.wait()
-    for copy in zs:
-        copy.wait()
-    for j in range(count):
-        for kind in (3, 2):
-            start(kind, 0, j)
     for packed in range(1, dp):
         top = packed.bit_length() - 1
-        for kind in (0, 1, 3, 2):
+        for kind in (0, 1):
             move(kind, packed & ~(1 << top), top).wait_recv()
             for j in range(top + 1, count):
                 start(kind, packed, j)
+    for copy in along:
+        copy.wait()
     for copy in started:
         copy.wait_send()
 
@@ -220,21 +222,24 @@
     rows, width = w_own.shape
     cut = width // 2 // LANES * LANES
     hbm = pl.BlockSpec(memory_space=pl.ANY)
+    dma = pltpu.SemaphoreType.DMA
     return pl.pallas_call(
         functools.partial(gather_weights, dp=dp, tp=tp, cut=cut),
         in_specs=[hbm] * 3,
         out_specs=(hbm,) * 3,
         out_shape=(
             sds((dp * rows, width), BF16),
-            sds((dp, tp) + st_own.shape, BF16),
-            sds((dp, tp) + sm_own.shape, F32),
+            sds((tp, dp) + st_own.shape, BF16),
+            sds((tp, dp) + sm_own.shape, F32),
         ),
         scratch_shapes=[
-            pltpu.SemaphoreType.DMA((3,)),
-            pltpu.SemaphoreType.DMA((2, tp)),
-            pltpu.SemaphoreType.DMA((2, tp)),
-            pltpu.SemaphoreType.DMA((4, dp)),
-            pltpu.SemaphoreType.DMA((4, dp)),
+            dma((3,)),
+            dma((2, dp)),
+            dma((2, dp)),
+            dma((2, tp)),
+            dma((2, tp)),
+            dma((2, dp)),
+            dma((2, dp)),
         ],
         compiler_params=pltpu.CompilerParams(collective_id=1, has_side_effects=True),
         name="gather_weights",
@@ -245,11 +250,13 @@
     return (a.astype(F32) + b.astype(F32)).astype(BF16)
 
 
-HALF = SPAN // 2
-
-
-def forward_step(f, x, c, w_v, ws_v, pv, saved, state_v, ext, stage, stats, sizes):
+PARTS = 4
+PART = SPAN // PARTS
+
+
+def forward_step(f, x, c, w_v, ws_v, pv, masks, saved, state_v, ext, stage, stats, sizes):
     inner, head_width, heads = sizes
+    lower_v, upper_v, marks_v, marks_t_v = masks
     cin_s, pre_s, gate_s, y_s, sp_s, state_s = saved
     states = ws_v.shape[1] // 2
     conv = inner + 2 * states
@@ -277,11 +284,10 @@
 
     rate = pv[7:8, 0:LANES]
     dt = softplus(step_in + pv[7:8, LANES : 2 * LANES])
-    total = mm_exact(causal_ones(True), dt * rate)
+    total = mm_ones(lower_v[...], dt * rate)
     total2 = total * LOG2E
     total2_t = jnp.transpose(total2)
-    marks = head_marks(head_width, inner)
-    marks2 = jnp.concatenate([marks, marks], 0)
+    marks2 = marks_v[...]
     end = total[SPAN - 1 : SPAN, :]
     xc = act[:, 0:inner]
     bmat = act[:, inner : inner + states].astype(BF16)
@@ -296,7 +302,7 @@
     keep = spread(jnp.broadcast_to(jnp.exp(end), (8, LANES)), marks2)[0:1, :]
     state_v[...] = keep * state + mm(jnp.transpose(bmat), weighted)
 
-    inter = mm_nt(cmat, bmat) * causal_ones(True)
+    inter = mm_nt(cmat, bmat) * lower_v[...].astype(F32)
     first, second = lane_masks()
     skip = pv[1:2, inner : 2 * inner]
     parts = []
@@ -326,9 +332,10 @@
 
 
 def backward_step(
-    f, x, c, w_v, ws_v, pv, totals, saved, dst_v, dext, small, grads, lowered_v, turned, put, between, stage, sizes, norm_width
+    f, x, c, w_v, ws_v, pv, masks, totals, saved, dst_v, dext, small, grads, lowered_v, turned, put, between, stage, sizes, norm_width
 ):
     inner, head_width, heads = sizes
+    lower_v, upper_v, marks_v, marks_t_v = masks
     cin_s, pre_s, gate_s, y_s, sp_s, state_s = saved
     states = ws_v.shape[1] // 2
     conv = inner + 2 * states
@@ -369,13 +376,11 @@
     rate = pv[7:8, 0:LANES]
     step_pre = sp_s[f] + pv[7:8, LANES : 2 * LANES]
     dt = softplus(step_pre)
-    total = mm_exact(causal_ones(True), dt * rate)
+    total = mm_ones(lower_v[...], dt * rate)
     total2 = total * LOG2E
     total2_t = jnp.transpose(total2)
-    marks = head_marks(head_width, inner)
-    marks2 = jnp.concatenate([marks, marks], 0)
-    marks_t = head_marks_t(head_width, inner)
-    marks_t2 = jnp.concatenate([marks_t, marks_t], 0)
+    marks2 = marks_v[...]
+    marks_t2 = marks_t_v[...]
     end = total[SPAN - 1 : SPAN, :]
     dt_wide = spread(dt, marks2)
     xd = (xc * dt_wide).astype(BF16)
@@ -397,7 +402,7 @@
     )
     dst_v[...] = keep * dst + mm(jnp.transpose(cmat), carried_grad)
 
-    causal = causal_ones(True)
+    causal = lower_v[...].astype(F32)
     inter = mm_nt(cmat, bmat) * causal
     first, second = lane_masks()
     inter_grad = jnp.zeros((SPAN, SPAN), F32)
@@ -423,7 +428,7 @@
 
     rows = gather_heads(yb_wide * y_scan - xd_wide * xd_grad, marks_t2)
     end_sum = gather_heads(jnp.broadcast_to(end_row, (8, inner)), marks_t2)[0:1, :]
-    decay_grad = mm_exact(causal_ones(False), rows) + end_sum
+    decay_grad = mm_ones(upper_v[...], rows) + end_sum
     dt_grad = decay_grad * rate + gather_heads(xc * xd_grad, marks_t2)
     small[7:8, 0:LANES] += jnp.sum(decay_grad * dt, axis=0, keepdims=True) * rate
     step_grad = dt_grad * sigmoid(step_pre)
@@ -519,6 +524,10 @@
     small2,
     small3,
     state_in,
+    lower_v,
+    upper_v,
+    marks_v,
+    marks_t_v,
     w_sem,
     load_sem,
     edge_send,
@@ -691,13 +700,13 @@
         return cycle * s + jnp.minimum(q, per) + jnp.maximum(q - per - 1, 0) // 2
 
     def combined(tick):
-        return jnp.maximum(3 * tick - 4, 0) // 7
+        return jnp.maximum(2 * tick - 2, 0) // 5
 
     def finished(tick):
-        return combined(jnp.maximum(tick - 4, 0))
+        return combined(jnp.maximum(tick - 3, 0))
 
     def sent(tick):
-        paced = jnp.minimum(made(jnp.maximum(tick, 1)), (3 * tick + 9) // 7)
+        paced = jnp.minimum(made(jnp.maximum(tick, 1)), (3 * tick + 4) // 7)
         return jnp.where(tick == ticks * sequences, pieces, jnp.where(tick < 1, 0, paced))
 
     def pump(tick):
@@ -705,29 +714,26 @@
         def _():
             @pl.loop(sent(tick - 1), sent(tick))
             def _(k):
-                for h in (0, 1):
+                for h in range(PARTS):
                     inward(k, h).start()
 
-        def middle(count, when, step):
-            @pl.when(is_middle & (when >= 1) & (count(when) > count(when - 1)))
-            def _():
-                for h in (0, 1):
-                    step(count(when) - 1, h)
-
-        middle(finished, tick - 1, end_finish)
-        middle(combined, tick - 1, end_combine)
-        middle(finished, tick, begin_finish)
-        middle(combined, tick, begin_combine)
+        @pl.when(is_middle & (finished(tick) > finished(tick - 1)))
+        def _():
+            finish(finished(tick) - 1)
+
+        @pl.when(is_middle & (combined(tick) > combined(tick - 1)))
+        def _():
+            combine(combined(tick) - 1)
 
     def combine(n, apart=False):
-        for group in ((0,), (1,)) if apart else ((0, 1),):
+        for group in zip(range(PARTS)) if apart else (range(PARTS),):
             for h in group:
                 begin_combine(n, h)
             for h in group:
                 end_combine(n, h)
 
     def finish(n, apart=False):
-        for group in ((0,), (1,)) if apart else ((0, 1),):
+        for group in zip(range(PARTS)) if apart else (range(PARTS),):
             for h in group:
                 begin_finish(n, h)
             for h in group:
@@ -769,6 +775,13 @@
     for copy in loads(0):
         copy.start()
     small[...] = jnp.zeros_like(small)
+    lower_v[...] = causal_ones(True)
+    upper_v[...] = causal_ones(False)
+    marks_v[0:LANES, :] = head_marks(head_width, inner)
+    marks_v[LANES:, :] = head_marks(head_width, inner)
+    marks_t_v[0:inner, :] = head_marks_t(head_width, inner)
+    marks_t_v[inner:, :] = head_marks_t(head_width, inner)
+    masks = (lower_v, upper_v, marks_v, marks_t_v)
     pl.semaphore_wait(barrier, len(greet))
     for copy in loads_w:
         copy.wait()
@@ -792,6 +805,7 @@
                 w_v,
                 ws_v,
                 pv,
+                masks,
                 saved,
                 state_v,
                 ext,
@@ -838,6 +852,7 @@
                 w_v,
                 ws_v,
                 pv,
+                masks,
                 totals[s, f],
                 saved,
                 dst_v,
@@ -855,28 +870,55 @@
             keep_piece(n)
             pump(tick + 2)
 
-    def to_sibling(q):
+    groups = ((0, 1024), (1024, wide - 1024), (wide, inner))
+    if wide <= 1024:
+        groups = ((0, wide), (wide, inner))
+
+    def to_sibling(q, g):
         at = pl.multiple_of((2 * q + 1 - parity) * rows, 16)
+        columns = pl.ds(*groups[g])
         return pltpu.make_async_remote_copy(
-            src_ref=wgrad.at[pl.ds(at, rows)],
-            dst_ref=rs1.at[q],
-            send_sem=rs1_send.at[q],
-            recv_sem=rs1_recv.at[q],
+            src_ref=wgrad.at[pl.ds(at, rows), columns],
+            dst_ref=rs1.at[q, :, columns],
+            send_sem=rs1_send.at[q, g],
+            recv_sem=rs1_recv.at[q, g],
             device_id=(sibling, z),
             device_id_type=MESH,
         )
 
-    def to_owner(k):
+    def to_owner(k, g):
         q = lax.rem(chip + k, half)
         at = pl.multiple_of((2 * q + parity) * rows, 16)
+        columns = pl.ds(*groups[g])
         return pltpu.make_async_remote_copy(
-            src_ref=wgrad.at[pl.ds(at, rows)],
-            dst_ref=rs2.at[chip],
-            send_sem=rs2_send.at[k],
-            recv_sem=rs2_recv.at[k],
+            src_ref=wgrad.at[pl.ds(at, rows), columns],
+            dst_ref=rs2.at[chip, :, columns],
+            send_sem=rs2_send.at[k, g],
+            recv_sem=rs2_recv.at[k, g],
             device_id=(2 * q + parity, z),
             device_id_type=MESH,
         )
+
+    def start_group(g):
+        @pl.loop(1, half + 1)
+        def _(k):
+            to_sibling(lax.rem(chip + k, half), g).start()
+
+    def pass_group(g):
+        columns = pl.ds(*groups[g])
+
+        @pl.loop(1, half)
+        def _(k):
+            q = lax.rem(chip + k, half)
+            to_sibling(q, g).wait_recv()
+            at = pl.multiple_of((2 * q + parity) * rows, 16)
+            block = wgrad[pl.ds(at, rows), columns].astype(F32) + fetch(rs1.at[q], g)
+            wgrad[pl.ds(at, rows), columns] = block.astype(BF16)
+            to_owner(k, g).start()
+
+        to_sibling(chip, g).wait_recv()
+        at = pl.multiple_of(me * rows, 16)
+        own[:, columns] = wgrad[pl.ds(at, rows), columns].astype(F32) + fetch(rs1.at[chip], g)
 
     def small_copy(source, target, index, device):
         return pltpu.make_async_remote_copy(
@@ -888,11 +930,12 @@
             device_id_type=MESH,
         )
 
-    def fetch(source):
-        copy = pltpu.make_async_copy(source, rsv, rs_sem.at[0])
+    def fetch(source, g):
+        columns = pl.ds(*groups[g])
+        copy = pltpu.make_async_copy(source.at[:, columns], rsv.at[:, columns], rs_sem.at[0])
         copy.start()
         copy.wait()
-        return rsv[...].astype(F32)
+        return rsv[:, columns].astype(F32)
 
     def left_operand(source):
         return [
@@ -905,16 +948,16 @@
             source.at[:, :, pl.ds(at, size)], tiles.at[slot, :, :, pl.ds(0, size)], tile_sem.at[slot]
         )
 
-    def products(source, width, place):
-        whole = width // 256
-
-        @pl.loop(0, whole)
+    def products(source, first, count, place):
+        tile_load(source, first * 256, 256, 0).start()
+
+        @pl.loop(0, count)
         def _(t):
             slot = lax.rem(t, 2)
-            at = pl.multiple_of(t * 256, 256)
+            at = pl.multiple_of((first + t) * 256, 256)
             tile_load(source, at, 256, slot).wait()
 
-            @pl.when(t + 1 < whole)
+            @pl.when(t + 1 < count)
             def _():
                 tile_load(source, pl.multiple_of(at + 256, 256), 256, 1 - slot).start()
 
@@ -926,34 +969,33 @@
     for copy in puts(per * (sequences - 1), (0, 1, 3)):
         copy.wait()
     last_tick = ticks * sequences
-    count = lambda tick: max(3 * tick - 4, 0) // 7
-    done_finish, done_combine = count(last_tick - 4), count(last_tick)
+    count = lambda tick: max(2 * tick - 2, 0) // 5
+    done_finish, done_combine = count(last_tick - 3), count(last_tick)
 
     @pl.when(is_middle)
     def _():
         store_piece(pieces - 1).wait()
-        for h in (0, 1):
-            if count(last_tick - 4) > count(last_tick - 5):
-                end_finish(done_finish - 1, h)
-            if count(last_tick) > count(last_tick - 1):
-                end_combine(done_combine - 1, h)
 
     for copy in left_operand(normed_hbm):
         copy.start()
-    tile_load(grads_hbm, 0, 256, 0).start()
     for copy in left_operand(normed_hbm):
         copy.wait()
-    products(grads_hbm, wide, 0)
-    rest = wide % 256
+    whole, rest = wide // 256, wide % 256
+    if len(groups) == 3:
+        products(grads_hbm, 0, 4, 0)
+        start_group(0)
+        products(grads_hbm, 4, whole - 4, 0)
+    else:
+        products(grads_hbm, 0, whole, 0)
     last = tile_load(grads_hbm, wide - rest, rest, 0)
     last.start()
     last.wait()
     wgrad[:, wide - rest : wide] = mm(
         w_v[:, 0:tokens], tiles[0].reshape(tokens, 256)[:, 0:rest]
     ).astype(BF16)
+    start_group(len(groups) - 2)
     for copy in left_operand(branch_hbm):
         copy.start()
-    tile_load(lowered_hbm, 0, 256, 0).start()
 
     steps, behind = [], done_finish
     for n in range(done_combine, pieces):
@@ -974,17 +1016,16 @@
         del steps[:count]
 
     drain(done_combine)
+    if len(groups) == 3:
+        pass_group(0)
     for copy in left_operand(branch_hbm):
         copy.wait()
-    products(lowered_hbm, inner, wide)
-
-    @pl.loop(0, half)
-    def _(q):
-        to_sibling(q).start()
-
+    products(lowered_hbm, 0, inner // 256, wide)
+    start_group(len(groups) - 1)
     first_small = small_copy(small, small1, 0, (sibling, z))
     first_small.start()
-    drain(done_combine + 2)
+    drain(done_combine + 1)
+    pass_group(len(groups) - 2)
     first_small.wait()
     small2[chip] = small[...] + small1[...]
     second_small = [
@@ -996,21 +1037,8 @@
     for copy in second_small:
         copy.start()
 
-    @pl.loop(1, half)
-    def _(k):
-        q = lax.rem(chip + k, half)
-        to_sibling(q).wait_recv()
-        at = pl.multiple_of((2 * q + parity) * rows, 16)
-        wgrad[pl.ds(at, rows), :] = (
-            wgrad[pl.ds(at, rows), :].astype(F32) + fetch(rs1.at[q])
-        ).astype(BF16)
-        to_owner(k).start()
-
-    drain(pieces - 2)
-    to_sibling(chip).wait_recv()
-    own[...] = wgrad[pl.ds(pl.multiple_of(me * rows, 16), rows), :].astype(F32) + fetch(
-        rs1.at[chip]
-    )
+    pass_group(len(groups) - 1)
+    drain(done_combine + 2)
     for copy in second_small:
         copy.wait()
     total = small2[0]
@@ -1023,12 +1051,14 @@
     ]
     for copy in third_small:
         copy.start()
-    drain(pieces - 1)
+    if done_combine + 2 < pieces - 3:
+        drain(pieces - 3)
 
     @pl.loop(1, half)
     def _(k):
-        to_owner(k).wait_recv()
-        own[...] += fetch(rs2.at[lax.rem(chip + half - k, half)])
+        for g in range(len(groups)):
+            to_owner(k, g).wait_recv()
+            own[:, pl.ds(*groups[g])] += fetch(rs2.at[lax.rem(chip + half - k, half)], g)
 
     share = state_sum.shape[0]
     state_columns = pl.ds(2 * inner, conv - inner)
@@ -1036,7 +1066,7 @@
     def state_rows(device):
         return pl.ds(pl.multiple_of(device * share, 8), share)
 
-    state_copies = [
+    state_copies = [] if share * tp != rows else [
         pltpu.make_async_remote_copy(
             src_ref=own.at[state_rows(flipped(z, k)), state_columns],
             dst_ref=state_in.at[k - 1],
@@ -1047,12 +1077,9 @@
         )
         for k in range(1, tp)
     ]
-    if share * tp == rows:
-        for copy in state_copies:
-            copy.start()
-    else:
-        state_copies = []
-
+    for copy in state_copies:
+        copy.start()
+    drain(pieces - 1)
     for copy in third_small:
         copy.wait()
     vectors[...] = jnp.zeros_like(vectors)
@@ -1067,10 +1094,8 @@
         vectors[5:6, depth + k * inner : depth + (k + 1) * inner] = small3[k, 1:2, 0:inner]
         head_sums[k, 0:1, :] = small3[k, 7:8, 0:LANES]
         head_sums[k, 1:2, :] = small3[k, 7:8, LANES : 2 * LANES]
-        marks_t = head_marks_t(head_width, inner)
         skips = gather_heads(
-            jnp.broadcast_to(small3[k, 1:2, inner : 2 * inner], (8, inner)),
-            jnp.concatenate([marks_t, marks_t], 0),
+            jnp.broadcast_to(small3[k, 1:2, inner : 2 * inner], (8, inner)), marks_t_v[...]
         )
         head_sums[k, 2:8, :] = skips[2:8, :]
     vectors[0:5, tp * inner : tp * inner + both] = shared
@@ -1088,16 +1113,18 @@
 
     @pl.loop(0, half)
     def _(q):
-        to_sibling(q).wait_send()
+        for g in range(len(groups)):
+            to_sibling(q, g).wait_send()
 
     @pl.loop(1, half)
     def _(k):
-        to_owner(k).wait_send()
+        for g in range(len(groups)):
+            to_owner(k, g).wait_send()
 
     @pl.when(is_middle)
     def _():
         for n in (pieces - 2, pieces - 1):
-            for h in (0, 1):
+            for h in range(PARTS):
                 across_copy(n, h).wait_send()
                 outward(n, h).wait_send()
                 kept(n, h).wait()
@@ -1106,7 +1133,7 @@
     def _():
         @pl.loop(0, pieces)
         def _(n):
-            for h in (0, 1):
+            for h in range(PARTS):
                 inward(n, h).wait_send()
                 outward(n, h).wait_recv()
 
@@ -1131,8 +1158,8 @@
         in_specs=[
             rows,
             rows,
-            pl.BlockSpec((1, 2, HALF, depth), lambda b: (b, 0, 0, 0)),
-            pl.BlockSpec((1, 2, HALF, depth), lambda b: (blocks + b, 0, 0, 0)),
+            pl.BlockSpec((1, PARTS, PART, depth), lambda b: (b, 0, 0, 0)),
+            pl.BlockSpec((1, PARTS, PART, depth), lambda b: (blocks + b, 0, 0, 0)),
             pl.BlockSpec((1, 1, 8, SPAN), lambda b: (b // per, b % per, 0, 0)),
         ],
         out_specs=(rows, rows),
@@ -1162,7 +1189,7 @@
     hbm = pl.BlockSpec(memory_space=pl.ANY)
     vmem = pl.BlockSpec(memory_space=pltpu.VMEM)
     dma = pltpu.SemaphoreType.DMA
-    piece = (2, HALF, depth)
+    piece = (PARTS, PART, depth)
     rows_of_x = (SPAN, depth)
     share = rows // tp if rows % (8 * tp) == 0 else 8
     flops = tokens * (6 * depth * (2 * inner + conv) + 6 * depth * inner + 80 * heads * SPAN * 64)
@@ -1219,21 +1246,25 @@
             pltpu.VMEM((half, 8, depth), F32),
             pltpu.VMEM((tp, 8, depth), F32),
             pltpu.VMEM((tp - 1, share, conv_states), F32),
+            pltpu.VMEM((SPAN, SPAN), BF16),
+            pltpu.VMEM((SPAN, SPAN), BF16),
+            pltpu.VMEM((2 * LANES, inner), BF16),
+            pltpu.VMEM((2 * inner, LANES), BF16),
             dma((2,)),
             dma((2, 2)),
-            dma((pieces, 2)),
-            dma((pieces, 2)),
-            dma((pieces, 2)),
-            dma((pieces, 2)),
-            dma((pieces, 2)),
+            dma((pieces, PARTS)),
+            dma((pieces, PARTS)),
+            dma((pieces, PARTS)),
+            dma((pieces, PARTS)),
+            dma((pieces, PARTS)),
             dma((1,)),
-            dma((3, 2)),
+            dma((3, PARTS)),
             dma((sequences, tp - 1)),
             dma((sequences, tp - 1)),
-            dma((half,)),
-            dma((half,)),
-            dma((half,)),
-            dma((half,)),
+            dma((half, 3)),
+            dma((half, 3)),
+            dma((half, 3)),
+            dma((half, 3)),
             dma((1,)),
             dma((4,)),
             dma((2 + blocks,)),
@@ -1323,8 +1354,8 @@
     flat = jnp.concatenate([conv_weight.reshape(-1), conv_bias, gain_vector])
     sm_own = pad_to(flat, -(-flat.shape[0] // 1024) * 1024).reshape(-1, LANES)
     w, st_full, sm_full = run_gather(w_own, st_own, sm_own, dp, tp)
-    ws = st_full[:, :, :state_rows].reshape(depth, conv_states)
-    small = sm_full.reshape(dp * tp, -1)
+    ws = st_full[:, :, :state_rows].swapaxes(0, 1).reshape(depth, conv_states)
+    small = sm_full.swapaxes(0, 1).reshape(dp * tp, -1)
     kernel_full = (
         small[:, : taps * conv_own].reshape(-1, taps, conv_own).transpose(1, 0, 2).reshape(taps, -1)
     )

time: 471 us -> 464 us (0.985)
  Pallas kernels: 443 us -> 433 us
    pallas_call x1, Pallas kernels: 372 us -> 361 us  [run_mixer(): pl.pallas_call(functools.partial(mixer, dp=dp, tp=tp, sizes=sizes, norm_w...]
where the time goes in v3:
time: 464 us; the launch traced here: 461 us
  Pallas kernels  433 us (93%)
  other arithmetic  18 us (4%)
  local copies, waits for them, and re-layouts  8.8 us (2%)
    pallas_call x1, Pallas kernels, run_mixer(): pl.pallas_call(functools.partial(mixer, dp=dp, tp=tp, sizes=sizes, norm_w...  361 us
    pallas_call x1, Pallas kernels, run_gather(): pl.pallas_call(functools.partial(gather_weights, dp=dp, tp=tp, cut=cut),...  54.7 us
    pallas_call x1, Pallas kernels, run_finalize(): pl.pallas_call(functools.partial(finalize, norm_width=norm_width), grid=(...  17 us
    sub x8, other arithmetic, adamw_update(): return (weight - step_rate * (update + decay_rate * weight), moment, square)  12.4 us

profile of v3, /device:TPU:0, one launch (start us, length us, event | category | flops | bytes accessed | tf_op | source)
XLA Modules:
  0.0 461.1 jit_solution(3514486650446147067)
XLA Ops:
  0.7 0.8 broadcast_multiply_fusion.1
  1.6 1.7 convert_element_type.26
  3.5 1.0 fusion.4.w_own
  4.5 0.6 convert_element_type.30.st_own
  5.2 0.7 fusion.13.sm_own
  5.9 54.7 %gather_weights.1 = (bf16[1536,2432]{1,0:T(8,128)(2,1)}, bf16[4,8,48,256]{3,2,1,0:T(8,128)(2,1)}, f32[4,8,8,128]{3,2,1,0:T(8,128)}) custom-call(bf16[192,2432]{1,0:T(8,128)(2,1)} %fusion.4.w_own, bf16[48,256]{1,0:T(8,128)(2,1)} %convert_element_type.30.st_own, f32[8,128]{1,0:T(8,128)} %fusion.13.sm_own), custom_call_target="tpu_custom_call" | custom-call | tf_op jit(solution)/shard_map/gather_weights/pallas_call | solution.py:226
  60.7 1.0 copy.82
  62.8 0.6 fusion.9.pv
  63.4 0.9 copy.81
  64.4 361.4 %mixer.1 = (bf16[16,4,64,1536]{3,2,1,0:T(8,128)(2,1)}, bf16[16,4,64,1536]{3,2,1,0:T(8,128)(2,1)}, bf16[16,4,64,1536]{3,2,1,0:T(8,128)(2,1)}, bf16[4,192,2688]{2,...) custom-call(bf16[2048,1536]{1,0:T(8,128)(2,1)} %x_ref.1, ...), custom_call_target="tpu_custom_call" | custom-call | flops 95026151424 | bytes 60000000 | tf_op jit(solution)/shard_map/mixer/pallas_call | solution.py:1196
  425.9 17.0 %finalize.1 = (bf16[2048,1536]{1,0:T(8,128)(2,1)}, f32[2048,1536]{1,0:T(8,128)}) custom-call(bf16[2048,1536]{1,0:T(8,128)(2,1)} %x_ref.1, bf16[2048,1536]{1,0:T(8,128)(2,1)} %c_ref.1, bf16[16,4,64,1536]{3,2,1,0:T(8,128)(2,1)} %get-tuple-element.40.out_ref.in_ref, bf16[16,4,64,1536]{3,2,1,0:T(8,128)(2,1)} %get-tuple-element.40.out_ref.in_ref, ...), custom_call_target="tpu_custom_call" | custom-call | flops 18874368 | bytes 44040192 | tf_op jit(solution)/shard_map/finalize/pallas_call | solution.py:1155
  442.9 0.8 constant_dynamic-slice_fusion
  443.7 0.6 add_subtract_fusion
  444.3 0.5 multiply_subtract_fusion.6
  444.8 0.8 constant_dynamic-slice_fusion.2
  445.6 0.6 multiply_subtract_fusion.5
  446.8 0.7 copy.90
  447.5 0.7 copy.91
  448.1 0.7 copy.92
  449.0 0.8 reshape.94
  450.2 6.6 %multiply_subtract_fusion = (f32[192,2,768]{2,1,0:T(2,128)}, f32[192,2,768]{2,1,0:T(2,128)}, f32[192,2,768]{2,1,0:T(2,128)}) fusion(f32[192,2,768]{2,1,0:T(2,128)S(1)} %copy-done, f32[192,2,768]{2,1,0:T(2,128)S(1)} %reshape.94, f32[192,2,768]{2,1,0:T(2,128)} %param.29, f32[192,2,768]{2,1,0:T(2,128)} %param.30), kind=kLoop, calls=%fused_computation.6 | loop fusion | flops 4423680 | bytes 8257536 | tf_op jit(solution)/shard_map/sub | solution.py:1290
  457.0 2.7 multiply_subtract_fusion.1
  459.7 0.7 multiply_subtract_fusion.3
  460.5 0.6 multiply_subtract_fusion.4
  (94 shorter events, 2.7 us)
Async XLA Ops:
  1.6 1.8 copy-start.1
  3.5 1.7 copy-start.17
  4.5 57.4 %copy-start.16 = (f32[3,48]{1,0:T(4,128)S(1)}, f32[3,48]{1,0:T(4,128)}, u32[]{:S(2)}) copy-start(f32[3,48]{1,0:T(4,128)} %param.49) | copy-start | bytes 1732
  60.7 2.8 copy-start.4
  425.8 17.9 %copy-start.19 = (f32[4,104]{1,0:T(4,128)S(1)}, f32[4,104]{1,0:T(4,128)}, u32[]{:S(2)}) copy-start(f32[4,104]{1,0:T(4,128)} %param.41) | copy-start | bytes 4996
  425.8 17.9 %copy-start.20 = (f32[4,104]{1,0:T(4,128)S(1)}, f32[4,104]{1,0:T(4,128)}, u32[]{:S(2)}) copy-start(f32[4,104]{1,0:T(4,128)} %param.42) | copy-start | bytes 4996
  425.8 18.5 %copy-start.26 = (f32[104]{0:T(128)S(1)}, f32[104]{0:T(128)}, u32[]{:S(2)}) copy-start(f32[104]{0:T(128)} %param.44) | copy-start | bytes 1252
  425.8 18.5 %copy-start.27 = (f32[104]{0:T(128)S(1)}, f32[104]{0:T(128)}, u32[]{:S(2)}) copy-start(f32[104]{0:T(128)} %param.45) | copy-start | bytes 1252
  425.8 19.8 %copy-start.24 = (f32[144]{0:T(256)S(1)}, f32[144]{0:T(256)}, u32[]{:S(2)}) copy-start(f32[144]{0:T(256)} %param.47) | copy-start | bytes 1732
  425.8 19.8 %copy-start.25 = (f32[144]{0:T(256)S(1)}, f32[144]{0:T(256)}, u32[]{:S(2)}) copy-start(f32[144]{0:T(256)} %param.48) | copy-start | bytes 1732
  425.9 20.5 %copy-start.13 = (f32[192,12]{0,1:T(8,128)S(1)}, f32[192,12]{0,1:T(8,128)}, u32[]{:S(2)}) copy-start(f32[192,12]{0,1:T(8,128)} %param.32) | copy-start | bytes 27652
  425.9 20.6 %copy-start.14 = (f32[192,12]{0,1:T(8,128)S(1)}, f32[192,12]{0,1:T(8,128)}, u32[]{:S(2)}) copy-start(f32[192,12]{0,1:T(8,128)} %param.33) | copy-start | bytes 27652
  425.9 20.7 %copy-start.9 = (f32[192,12]{0,1:T(8,128)S(1)}, f32[192,12]{0,1:T(8,128)}, u32[]{:S(2)}) copy-start(f32[192,12]{0,1:T(8,128)} %param.31) | copy-start | bytes 27652
  425.9 20.8 %copy-start.3 = (f32[192,2688]{1,0:T(8,128)S(1)}, f32[192,2688]{1,0:T(8,128)}, u32[]{:S(2)}) copy-start(f32[192,2688]{1,0:T(8,128)} %get-tuple-element.44) | copy-start | bytes 6193156
  450.2 6.6 %copy-start.2 = (f32[768,192]{0,1:T(8,128)S(1)}, f32[768,192]{0,1:T(8,128)}, u32[]{:S(2)}) copy-start(f32[768,192]{0,1:T(8,128)} %param.34) | copy-start | bytes 1769476
  450.2 6.6 %copy-start.5 = (f32[768,192]{0,1:T(8,128)S(1)}, f32[768,192]{0,1:T(8,128)}, u32[]{:S(2)}) copy-start(f32[768,192]{0,1:T(8,128)} %param.35) | copy-start | bytes 1769476
  450.2 6.6 %copy-start.6 = (f32[768,192]{0,1:T(8,128)S(1)}, f32[768,192]{0,1:T(8,128)}, u32[]{:S(2)}) copy-start(f32[768,192]{0,1:T(8,128)} %param.36) | copy-start | bytes 1769476
  456.9 2.8 copy-start.8
  456.9 2.8 copy-start.10
  456.9 2.8 copy-start.11
  456.9 2.7 copy-start.12
  456.9 3.4 copy-start.18
  456.9 3.5 copy-start.21
  457.0 3.5 copy-start.22
  (4 other events, 5.7 us)

commit v4 on v3

--- a/solution.py
+++ b/solution.py
@@ -136,7 +136,7 @@
     pl.semaphore_wait(barrier, dp + tp - 2)
 
     orders = axis_bits(dp)
-    parts = (pl.ds(0, cut), pl.ds(cut, width - cut))
+    parts = ((0, cut), (cut, rows - cut))
 
     def row_of(mask):
         return pl.multiple_of(flipped(me, mask) * rows, 16)
@@ -145,12 +145,12 @@
         return sum(1 << bits[j] for j in range(count) if packed >> j & 1)
 
     def move(kind, packed, j):
-        bits, columns = orders[kind], parts[kind]
+        bits, (offset, size) = orders[kind], parts[kind]
         mask = full_mask(bits, packed)
         slot = packed | (1 << j)
-        place = w_full.at[pl.ds(row_of(mask), rows), columns]
+        place = w_full.at[pl.ds(pl.multiple_of(row_of(mask) + offset, 16), size)]
         return pltpu.make_async_remote_copy(
-            src_ref=w_own.at[:, columns] if mask == 0 else place,
+            src_ref=w_own.at[pl.ds(offset, size)] if mask == 0 else place,
             dst_ref=place,
             send_sem=send_sem.at[kind, slot],
             recv_sem=recv_sem.at[kind, slot],
@@ -220,7 +220,7 @@
 
 def run_gather(w_own, st_own, sm_own, dp, tp):
     rows, width = w_own.shape
-    cut = width // 2 // LANES * LANES
+    cut = rows // 2 // 16 * 16
     hbm = pl.BlockSpec(memory_space=pl.ANY)
     dma = pltpu.SemaphoreType.DMA
     return pl.pallas_call(

time: 464 us -> 464 us (level)
  no operation moved by 1% of the time
where the time goes in v4:
time: 464 us; the launch traced here: 461 us
  Pallas kernels  433 us (93%)
  other arithmetic  18 us (4%)
  local copies, waits for them, and re-layouts  8.8 us (2%)
    pallas_call x1, Pallas kernels, run_mixer(): pl.pallas_call(functools.partial(mixer, dp=dp, tp=tp, sizes=sizes, norm_w...  361 us
    pallas_call x1, Pallas kernels, run_gather(): pl.pallas_call(functools.partial(gather_weights, dp=dp, tp=tp, cut=cut),...  54.7 us
    pallas_call x1, Pallas kernels, run_finalize(): pl.pallas_call(functools.partial(finalize, norm_width=norm_width), grid=(...  17 us
    sub x8, other arithmetic, adamw_update(): return (weight - step_rate * (update + decay_rate * weight), moment, square)  12.4 us

profile of v4, /device:TPU:0, one launch (start us, length us, event | category | flops | bytes accessed | tf_op | source)
XLA Modules:
  0.0 461.1 jit_solution(2691345723219460271)
XLA Ops:
  0.7 0.8 broadcast_multiply_fusion.1
  1.6 1.7 convert_element_type.26
  3.5 1.0 fusion.4.w_own
  4.5 0.6 convert_element_type.30.st_own
  5.2 0.7 fusion.13.sm_own
  5.9 54.7 %gather_weights.1 = (bf16[1536,2432]{1,0:T(8,128)(2,1)}, bf16[4,8,48,256]{3,2,1,0:T(8,128)(2,1)}, f32[4,8,8,128]{3,2,1,0:T(8,128)}) custom-call(bf16[192,2432]{1,0:T(8,128)(2,1)} %fusion.4.w_own, bf16[48,256]{1,0:T(8,128)(2,1)} %convert_element_type.30.st_own, f32[8,128]{1,0:T(8,128)} %fusion.13.sm_own), custom_call_target="tpu_custom_call" | custom-call | tf_op jit(solution)/shard_map/gather_weights/pallas_call | solution.py:226
  60.7 1.0 copy.82
  62.8 0.6 fusion.9.pv
  63.4 0.9 copy.81
  64.4 361.4 %mixer.1 = (bf16[16,4,64,1536]{3,2,1,0:T(8,128)(2,1)}, bf16[16,4,64,1536]{3,2,1,0:T(8,128)(2,1)}, bf16[16,4,64,1536]{3,2,1,0:T(8,128)(2,1)}, bf16[4,192,2688]{2,...) custom-call(bf16[2048,1536]{1,0:T(8,128)(2,1)} %x_ref.1, ...), custom_call_target="tpu_custom_call" | custom-call | flops 95026151424 | bytes 60000000 | tf_op jit(solution)/shard_map/mixer/pallas_call | solution.py:1196
  425.9 17.0 %finalize.1 = (bf16[2048,1536]{1,0:T(8,128)(2,1)}, f32[2048,1536]{1,0:T(8,128)}) custom-call(bf16[2048,1536]{1,0:T(8,128)(2,1)} %x_ref.1, bf16[2048,1536]{1,0:T(8,128)(2,1)} %c_ref.1, bf16[16,4,64,1536]{3,2,1,0:T(8,128)(2,1)} %get-tuple-element.40.out_ref.in_ref, bf16[16,4,64,1536]{3,2,1,0:T(8,128)(2,1)} %get-tuple-element.40.out_ref.in_ref, ...), custom_call_target="tpu_custom_call" | custom-call | flops 18874368 | bytes 44040192 | tf_op jit(solution)/shard_map/finalize/pallas_call | solution.py:1155
  442.9 0.8 constant_dynamic-slice_fusion
  443.7 0.6 add_subtract_fusion
  444.3 0.5 multiply_subtract_fusion.6
  444.8 0.8 constant_dynamic-slice_fusion.2
  445.6 0.6 multiply_subtract_fusion.5
  446.8 0.7 copy.90
  447.5 0.7 copy.91
  448.2 0.7 copy.92
  449.0 0.8 reshape.94
  450.3 6.6 %multiply_subtract_fusion = (f32[192,2,768]{2,1,0:T(2,128)}, f32[192,2,768]{2,1,0:T(2,128)}, f32[192,2,768]{2,1,0:T(2,128)}) fusion(f32[192,2,768]{2,1,0:T(2,128)S(1)} %copy-done, f32[192,2,768]{2,1,0:T(2,128)S(1)} %reshape.94, f32[192,2,768]{2,1,0:T(2,128)} %param.29, f32[192,2,768]{2,1,0:T(2,128)} %param.30), kind=kLoop, calls=%fused_computation.6 | loop fusion | flops 4423680 | bytes 8257536 | tf_op jit(solution)/shard_map/sub | solution.py:1290
  457.0 2.7 multiply_subtract_fusion.1
  459.7 0.7 multiply_subtract_fusion.3
  460.5 0.6 multiply_subtract_fusion.4
  (94 shorter events, 2.7 us)
Async XLA Ops:
  1.6 1.8 copy-start.1
  3.5 1.7 copy-start.17
  4.5 57.4 %copy-start.16 = (f32[3,48]{1,0:T(4,128)S(1)}, f32[3,48]{1,0:T(4,128)}, u32[]{:S(2)}) copy-start(f32[3,48]{1,0:T(4,128)} %param.49) | copy-start | bytes 1732
  60.6 2.8 copy-start.4
  425.8 17.9 %copy-start.19 = (f32[4,104]{1,0:T(4,128)S(1)}, f32[4,104]{1,0:T(4,128)}, u32[]{:S(2)}) copy-start(f32[4,104]{1,0:T(4,128)} %param.41) | copy-start | bytes 4996
  425.8 17.9 %copy-start.20 = (f32[4,104]{1,0:T(4,128)S(1)}, f32[4,104]{1,0:T(4,128)}, u32[]{:S(2)}) copy-start(f32[4,104]{1,0:T(4,128)} %param.42) | copy-start | bytes 4996
  425.8 18.5 %copy-start.26 = (f32[104]{0:T(128)S(1)}, f32[104]{0:T(128)}, u32[]{:S(2)}) copy-start(f32[104]{0:T(128)} %param.44) | copy-start | bytes 1252
  425.8 18.5 %copy-start.27 = (f32[104]{0:T(128)S(1)}, f32[104]{0:T(128)}, u32[]{:S(2)}) copy-start(f32[104]{0:T(128)} %param.45) | copy-start | bytes 1252
  425.9 19.8 %copy-start.24 = (f32[144]{0:T(256)S(1)}, f32[144]{0:T(256)}, u32[]{:S(2)}) copy-start(f32[144]{0:T(256)} %param.47) | copy-start | bytes 1732
  425.9 19.8 %copy-start.25 = (f32[144]{0:T(256)S(1)}, f32[144]{0:T(256)}, u32[]{:S(2)}) copy-start(f32[144]{0:T(256)} %param.48) | copy-start | bytes 1732
  425.9 20.5 %copy-start.13 = (f32[192,12]{0,1:T(8,128)S(1)}, f32[192,12]{0,1:T(8,128)}, u32[]{:S(2)}) copy-start(f32[192,12]{0,1:T(8,128)} %param.32) | copy-start | bytes 27652
  425.9 20.6 %copy-start.14 = (f32[192,12]{0,1:T(8,128)S(1)}, f32[192,12]{0,1:T(8,128)}, u32[]{:S(2)}) copy-start(f32[192,12]{0,1:T(8,128)} %param.33) | copy-start | bytes 27652
  425.9 20.7 %copy-start.9 = (f32[192,12]{0,1:T(8,128)S(1)}, f32[192,12]{0,1:T(8,128)}, u32[]{:S(2)}) copy-start(f32[192,12]{0,1:T(8,128)} %param.31) | copy-start | bytes 27652
  425.9 20.8 %copy-start.3 = (f32[192,2688]{1,0:T(8,128)S(1)}, f32[192,2688]{1,0:T(8,128)}, u32[]{:S(2)}) copy-start(f32[192,2688]{1,0:T(8,128)} %get-tuple-element.44) | copy-start | bytes 6193156
  450.3 6.6 %copy-start.2 = (f32[768,192]{0,1:T(8,128)S(1)}, f32[768,192]{0,1:T(8,128)}, u32[]{:S(2)}) copy-start(f32[768,192]{0,1:T(8,128)} %param.34) | copy-start | bytes 1769476
  450.3 6.6 %copy-start.5 = (f32[768,192]{0,1:T(8,128)S(1)}, f32[768,192]{0,1:T(8,128)}, u32[]{:S(2)}) copy-start(f32[768,192]{0,1:T(8,128)} %param.35) | copy-start | bytes 1769476
  450.3 6.6 %copy-start.6 = (f32[768,192]{0,1:T(8,128)S(1)}, f32[768,192]{0,1:T(8,128)}, u32[]{:S(2)}) copy-start(f32[768,192]{0,1:T(8,128)} %param.36) | copy-start | bytes 1769476
  456.9 2.8 copy-start.8
  456.9 2.8 copy-start.10
  456.9 2.8 copy-start.11
  456.9 2.7 copy-start.12
  457.0 3.4 copy-start.18
  457.0 3.5 copy-start.21
  457.0 3.5 copy-start.22
  (4 other events, 5.7 us)
